TPU v7x, 256 devices: a whole 4x4x8 slice. The times are simulated.
256 devices in a mesh: dp: 16 (over z, x_hi), tensor: 16 (over y, x_lo, core).
Axes of the slice: x: 4 (x_hi: 2, x_lo: 2; x = x_hi * 2 + x_lo), y: 4, z: 8, core: 2. Of those that a mesh axis runs over, the one named last changes fastest.
Arguments:
- queries: bfloat16 [8192, 8192], P('dp', 'tensor'), may hold values from -20 to 20
- keys: bfloat16 [8192, 8192], P('dp', 'tensor'), may hold values from -20 to 20
- values: bfloat16 [8192, 8192], P('dp', 'tensor'), may hold values from -6 to 6
- out_grad: bfloat16 [8192, 8192], P('dp'), may hold values from -6 to 6
- o_weight: bfloat16 [8192, 8192], P('tensor', 'dp'), may hold values from -0.0625 to 0.0625
- exponents: int32 [8192], P('tensor'), may hold values from -2 to 2
- valid_lengths: int32 [16], P('dp'), may hold values from 128 to 512, as said below
Outputs:
- grad_queries: bfloat16 [8192, 8192], P('dp', 'tensor')
- grad_keys: bfloat16 [8192, 8192], P('dp', 'tensor')
- grad_values: bfloat16 [8192, 8192], P('dp', 'tensor')
- grad_weight: float32 [8192, 8192], P('tensor', 'dp')
Inputs may be any that keep to these rules, and one draw needn't show every extreme that they name: `valid_lengths`: each block has at least 128 valid tokens; some block is full and some has exactly 128.
All inputs are finite; a program needn't handle non-finite values.
Results may differ from a plain program's by a relative error of at most 0.024.
Values may be sent and summed in bfloat16 or wider, within the bound.
No kernel may reach another device: no remote copies, remote signals or barrier semaphores. Data moves between devices by JAX's collectives and lax.ppermute only.
A program may use at most 128 MiB of HBM per device.

v0:
```python
import math

import jax
import jax.numpy as jnp
from jax import lax
from jax.sharding import PartitionSpec as P

HEADS = 64
HEAD_DIM = 128


def sylvester(count):
    labels = jnp.arange(count, dtype=jnp.int32)
    common = labels[:, None] & labels[None, :]
    parity = jnp.zeros((count, count), jnp.int32)
    for bit_number in range(count.bit_length() - 1):
        parity = parity ^ common >> bit_number & 1
    return (1 - 2 * parity).astype(jnp.bfloat16)


def rotate_pair(first, second):
    norm_scale = 1.0 / math.sqrt(HEADS)
    local_count = first.shape[1]
    table = sylvester(local_count * lax.axis_size("tensor"))

    def mix_one(gathered):
        mixed = jnp.einsum("gh,thc->tgc", table, gathered, preferred_element_type=jnp.float32)
        rounded = (mixed * norm_scale).astype(jnp.bfloat16)
        return lax.all_to_all(rounded, "tensor", split_axis=1, concat_axis=0, tiled=True)

    def rotate_one(blocks):
        return mix_one(lax.all_to_all(blocks, "tensor", split_axis=0, concat_axis=1, tiled=True))

    return (rotate_one(first), rotate_one(second))


def attention_probs(query_heads, key_heads, length):
    count = query_heads.shape[0]
    score_scale = 1.0 / math.sqrt(query_heads.shape[2])
    scores = (
        jnp.einsum("thc,shc->hts", query_heads, key_heads, preferred_element_type=jnp.float32)
        * score_scale
    )
    places = jnp.arange(count, dtype=jnp.int32)
    allowed = (places[None, :] <= places[:, None]) & (places[None, :] < length)
    scores = jnp.where(allowed[None, :, :], scores, -1e30)
    top = jnp.max(scores, axis=-1, keepdims=True)
    weights = jnp.exp(scores - top)
    return weights / jnp.sum(weights, axis=-1, keepdims=True)


def body(queries, keys, values, out_grad, o_weight, exponents, valid_lengths):
    tok_rows = queries.shape[0]
    local_heads = queries.shape[1] // HEAD_DIM
    head_shape = (tok_rows, local_heads, HEAD_DIM)
    query_heads = queries.reshape(head_shape)
    key_heads = keys.reshape(head_shape)
    value_heads = values.reshape(head_shape)
    probs = attention_probs(query_heads, key_heads, valid_lengths[0])
    probs_low = probs.astype(jnp.bfloat16)
    attended = jnp.einsum(
        "hts,shc->thc", probs_low, value_heads, preferred_element_type=jnp.float32
    ).astype(jnp.bfloat16)
    channel_scale = jnp.exp2(exponents.astype(jnp.float32))
    columns = out_grad
    projected = lax.dot_general(
        columns,
        lax.all_gather(o_weight, "dp", axis=1, tiled=True),
        (((1,), (1,)), ((), ())),
        preferred_element_type=jnp.float32,
    )
    grad_rotated = (projected * channel_scale[None, :]).astype(jnp.bfloat16)
    rotated_heads, grad_attended = rotate_pair(attended, grad_rotated.reshape(head_shape))
    rotated = rotated_heads.reshape(tok_rows, -1)
    grad_value = jnp.einsum(
        "hts,thc->shc", probs_low, grad_attended, preferred_element_type=jnp.float32
    ).astype(jnp.bfloat16)
    grad_probs = jnp.einsum(
        "thc,shc->hts", grad_attended, value_heads, preferred_element_type=jnp.float32
    )
    centre = jnp.sum(probs * grad_probs, axis=-1, keepdims=True)
    grad_scores = (probs * (grad_probs - centre) / math.sqrt(HEAD_DIM)).astype(jnp.bfloat16)
    grad_query = jnp.einsum(
        "hts,shc->thc", grad_scores, key_heads, preferred_element_type=jnp.float32
    ).astype(jnp.bfloat16)
    grad_key = jnp.einsum(
        "hts,thc->shc", grad_scores, query_heads, preferred_element_type=jnp.float32
    ).astype(jnp.bfloat16)
    columns = out_grad
    summed = lax.psum_scatter(
        lax.dot_general(
            columns, rotated, (((0,), (0,)), ((), ())), preferred_element_type=jnp.float32
        ).astype(jnp.bfloat16),
        "dp",
        scatter_dimension=0,
        tiled=True,
    ).astype(jnp.float32)
    grad_weight = summed.T * channel_scale[:, None]
    return (
        grad_query.reshape(tok_rows, -1),
        grad_key.reshape(tok_rows, -1),
        grad_value.reshape(tok_rows, -1),
        grad_weight,
    )


def solution(mesh):
    return jax.shard_map(
        body,
        mesh=mesh,
        in_specs=(
            P("dp", "tensor"),
            P("dp", "tensor"),
            P("dp", "tensor"),
            P("dp", None),
            P("tensor", "dp"),
            P("tensor"),
            P("dp"),
        ),
        out_specs=(P("dp", "tensor"), P("dp", "tensor"), P("dp", "tensor"), P("tensor", "dp")),
        check_vma=False,
    )
```

profile of v0, /device:TPU:1, one launch (start us, length us, event | category | flops | bytes accessed | tf_op | source)
XLA Modules:
  0.0 405.5 jit_solution(8187142413333433596)
XLA Ops:
  7.2 0.7 all-gather.2.cloned.1.call-update
  8.0 1.3 copy.75
  9.9 1.3 copy.76
  11.3 3.6 fusion.69
  14.9 3.2 fusion.27
  18.2 0.4 copy.63
  18.6 20.5 %all_to_all.69 = bf16[512,4,128]{2,1,0:T(4,128)(2,1)S(1)} all-to-all(bf16[512,4,128]{2,1,0:T(4,128)(2,1)S(1)} %copy.63), channel_id=1, replica_groups=mesh['dp'=16,'tensor'=16] {'tensor'}, dimensions={0} | all-to-all | bytes 1048576 | tf_op jit(solution)/shard_map/all_to_all | solution.py:32
  40.0 14.0 %all_to_all.70 = bf16[32,64,128]{2,0,1:T(8,128)(2,1)S(1)} all-to-all(bf16[32,64,128]{2,0,1:T(8,128)(2,1)S(1)} %copy.65), channel_id=1, replica_groups=mesh['dp'=16,'tensor'=16] {'tensor'}, dimensions={1} | all-to-all | bytes 1048576 | tf_op jit(solution)/shard_map/all_to_all | solution.py:29
  54.4 7.0 %fusion.2 = bf16[8192,512]{0,1:T(8,128)(2,1)} fusion(bf16[512,8192]{1,0:T(8,128)(2,1)S(1)} %bitcast.73, bf16[64,8,4,128]{3,2,1,0:T(4,128)(2,1)S(1)} %bitcast.76), kind=kOutput, calls=%fused_computation.3 | convolution fusion | flops 4299161600 | bytes 17301504 | tf_op jit(solution)/shard_map/dot_general | solution.py:91
  61.4 0.7 copy-done.1
  62.1 103.3 %all-gather.2.cloned.1.call-done = bf16[512,8192]{1,0:T(8,128)(2,1)} async-done(((bf16[512,512]{1,0:T(8,128)(2,1)}), bf16[512,8192]{1,0:T(8,128)(2,1)}) %all-gather.2.cloned.1.call-update) | async-done | bytes 8388624 | tf_op jit(solution)/shard_map/all_gather | solution.py:68
  165.4 10.3 %fusion.26 = bf16[512,512]{0,1:T(8,128)(2,1)S(1)} fusion(bf16[512,8192]{1,0:T(8,128)(2,1)} %param.10, bf16[512,8192]{1,0:T(8,128)(2,1)} %all-gather.2.cloned.1.call-done, f32[512]{0:T(512)S(1)} %multiply_exponential_fusion), kind=kOutput, calls=%fused_computation.27 | convolution fusion | flops 4295491584 | bytes 17303552 | tf_op jit(solution)/shard_map/dot_general | solution.py:66
  176.0 19.6 %all_to_all.71 = bf16[512,4,128]{2,1,0:T(4,128)(2,1)S(1)} all-to-all(bf16[512,4,128]{2,1,0:T(4,128)(2,1)S(1)} %copy.49), channel_id=1, replica_groups=mesh['dp'=16,'tensor'=16] {'tensor'}, dimensions={0} | all-to-all | bytes 1048576 | tf_op jit(solution)/shard_map/all_to_all | solution.py:32
  195.6 0.4 copy.51
  196.7 12.9 %all_to_all.72 = bf16[32,64,128]{2,0,1:T(8,128)(2,1)S(1)} all-to-all(bf16[32,64,128]{2,0,1:T(8,128)(2,1)S(1)} %copy.52), channel_id=1, replica_groups=mesh['dp'=16,'tensor'=16] {'tensor'}, dimensions={1} | all-to-all | bytes 1048576 | tf_op jit(solution)/shard_map/all_to_all | solution.py:29
  209.6 2.7 fusion.36
  212.3 8.2 %fusion.20 = bf16[4,512,128]{1,2,0:T(8,128)(2,1)S(1)} fusion(bf16[512,4,128]{0,2,1:T(8,128)(2,1)S(1)} %bitcast.86, f32[4,512,512]{1,2,0:T(8,128)} %fusion.36, f32[4,512,512]{1,2,0:T(8,128)} %get-tuple-element.17, f32[4,512]{1,0:T(4,128)S(1)} %get-tuple-element.16), kind=kOutput, calls=%fused_computation.25 | convolution fusion | flops 276040192 | bytes 9445376 | tf_op jit(solution)/shard_map/hts,shc->thc/dot_general | solution.py:83
  220.6 1.0 copy.67
  221.6 7.7 %fusion.23 = bf16[4,512,128]{1,2,0:T(8,128)(2,1)S(1)} fusion(bf16[512,4,128]{0,2,1:T(8,128)(2,1)S(1)} %bitcast.84, f32[4,512,512]{1,2,0:T(8,128)} %fusion.36, f32[4,512,512]{1,2,0:T(8,128)} %get-tuple-element.17, f32[4,512]{1,0:T(4,128)S(1)} %get-tuple-element.16), kind=kOutput, calls=%fused_computation.26 | convolution fusion | flops 276040192 | bytes 9445376 | tf_op jit(solution)/shard_map/hts,thc->shc/dot_general | solution.py:86
  229.2 1.0 copy.68
  230.3 3.1 convolution_convert_fusion.2
  233.4 1.0 copy.69
  234.4 162.1 %reduce-scatter.2.cloned.1.call-done = bf16[512,512]{0,1:T(8,128)(2,1)} async-done(((bf16[8192,512]{0,1:T(8,128)(2,1)}), bf16[512,512]{0,1:T(8,128)(2,1)}) %reduce-scatter.2.cloned.1.call-update) | async-done | bytes 524304 | tf_op jit(solution)/shard_map/reduce_scatter | solution.py:90
  396.5 2.1 multiply_bitcast_fusion
  (23 shorter events, 2.5 us)
Async XLA Ops:
  7.2 7.8 %copy-start = (bf16[512,512]{1,0:T(8,128)(2,1)S(1)}, bf16[512,512]{1,0:T(8,128)(2,1)}, u32[]{:S(2)}) copy-start(bf16[512,512]{1,0:T(8,128)(2,1)} %param.9) | copy-start | bytes 1572868
  7.2 158.2 %all-gather.2.cloned.1.call-start = ((), (), s32[]{:S(2)}) async-start(), calls=%async_computation.5 | async-start | bytes 8912896 | tf_op jit(solution)/shard_map/all_gather | solution.py:68
  7.9 388.6 %reduce-scatter.2.cloned.1.call-start = ((), (), s32[]{:S(2)}) async-start(), calls=%async_computation.6 | async-start | bytes 8912896 | tf_op jit(solution)/shard_map/reduce_scatter | solution.py:90
  14.9 39.4 %slice-start = ((s8[8388608]{0:T(1024)(128)(4,1)}), s8[4194304]{0:T(1024)(128)(4,1)S(1)}, s32[]{:S(2)}) async-start(s8[8388608]{0:T(1024)(128)(4,1)} %bitcast.72), calls=%async_computation.7 | async-start | bytes 8388608
  14.9 39.4 %slice-start.1 = ((s8[8388608]{0:T(1024)(128)(4,1)}), s8[4194304]{0:T(1024)(128)(4,1)S(1)}, s32[]{:S(2)}) async-start(s8[8388608]{0:T(1024)(128)(4,1)} %bitcast.72), calls=%async_computation.8 | async-start | bytes 8388608
  61.4 0.7 copy-start.1
Sparse Core Ops, SparseCore 0:
  10.5 154.8 all-gather.1
  169.5 226.9 reduce-scatter.1
where the time goes:
time: 409 us; the launch traced here: 405 us
  waiting for transfers between devices  266 us (65%)
  blocking collectives  67 us (16%)
  matrix products  46.5 us (11%)
  between operations  14.9 us (4%)
  local copies, waits for them, and re-layouts  8.66 us (2%)
    reduce_scatter x1, waiting for transfers between devices, body(): lax.psum_scatter(lax.dot_general(columns, rotated, (((0,), (0,)), ((), ()...  162 us
    all_gather x1, waiting for transfers between devices, body(): lax.all_gather(o_weight, 'dp', axis=1, tiled=True)  103 us
    all_to_all x2, blocking collectives, rotate_one(): lax.all_to_all(blocks, 'tensor', split_axis=0, concat_axis=1, tiled=True)  40.1 us
    all_to_all x2, blocking collectives, mix_one(): lax.all_to_all(rounded, 'tensor', split_axis=1, concat_axis=0, tiled=True)  26.9 us
    dot_general x1, matrix products, body(): lax.dot_general(columns, lax.all_gather(o_weight, 'dp', axis=1, tiled=Tru...  10.3 us
    dot_general x1, matrix products, body(): jnp.einsum('hts,shc->thc', grad_scores, key_heads, preferred_element_type...  8.25 us
  transfers between devices with their start and end apart: 2, of which 2 were waited for; matrix products, arithmetic and copies ran while one was open for 13% of the time, Pallas kernels for 0%

commit v1 on v0

v1 whole, which is shorter than its diff:
```python
import functools
import math

import jax
import jax.numpy as jnp
from jax import lax
from jax.experimental import pallas as pl
from jax.experimental.pallas import tpu as pltpu
from jax.sharding import Mesh
from jax.sharding import PartitionSpec as P

HEADS = 64
HEAD_DIM = 128
DP = ("z", "xh")
TENSOR = ("y", "xl", "co")
BLK = 512
VMEM_LIMIT = 48 * 1024 * 1024


def params():
    return pltpu.CompilerParams(vmem_limit_bytes=VMEM_LIMIT)


def dot(a, b, ca, cb):
    return lax.dot_general(a, b, (((ca,), (cb,)), ((), ())), preferred_element_type=jnp.float32)


def fwd_kernel(len_ref, q_ref, k_ref, v_ref, att_ref, p_ref):
    scores = dot(q_ref[...], k_ref[...], 1, 1) * (1.0 / math.sqrt(HEAD_DIM))
    t = lax.broadcasted_iota(jnp.int32, scores.shape, 0)
    s = lax.broadcasted_iota(jnp.int32, scores.shape, 1)
    scores = jnp.where((s <= t) & (s < len_ref[0]), scores, -1e30)
    top = jnp.max(scores, axis=-1, keepdims=True)
    weights = jnp.exp(scores - top)
    probs = weights / jnp.sum(weights, axis=-1, keepdims=True)
    p_ref[0] = probs
    att_ref[...] = dot(probs.astype(jnp.bfloat16), v_ref[...], 1, 0).astype(jnp.bfloat16)


def attention_fwd(length, q, k, v):
    heads = q.shape[1] // HEAD_DIM
    head = pl.BlockSpec((BLK, HEAD_DIM), lambda h, *_: (0, h))
    return pl.pallas_call(
        fwd_kernel,
        grid_spec=pltpu.PrefetchScalarGridSpec(
            num_scalar_prefetch=1,
            grid=(heads,),
            in_specs=[head, head, head],
            out_specs=[head, pl.BlockSpec((1, BLK, BLK), lambda h, *_: (h, 0, 0))],
        ),
        out_shape=[
            jax.ShapeDtypeStruct(q.shape, jnp.bfloat16),
            jax.ShapeDtypeStruct((heads, BLK, BLK), jnp.float32),
        ],
        compiler_params=params(),
        cost_estimate=pl.CostEstimate(
            flops=heads * 4 * BLK * BLK * HEAD_DIM, bytes_accessed=8 << 20, transcendentals=heads * BLK * BLK
        ),
        name="attention_fwd",
    )(length, q, k, v)


def bwd_kernel(p_ref, q_ref, k_ref, v_ref, g_ref, dq_ref, dk_ref, dv_ref):
    probs = p_ref[0]
    grad = g_ref[...]
    dv_ref[...] = dot(probs.astype(jnp.bfloat16), grad, 0, 0).astype(jnp.bfloat16)
    grad_probs = dot(grad, v_ref[...], 1, 1)
    centre = jnp.sum(probs * grad_probs, axis=-1, keepdims=True)
    grad_scores = (probs * (grad_probs - centre) * (1.0 / math.sqrt(HEAD_DIM))).astype(jnp.bfloat16)
    dq_ref[...] = dot(grad_scores, k_ref[...], 1, 0).astype(jnp.bfloat16)
    dk_ref[...] = dot(grad_scores, q_ref[...], 0, 0).astype(jnp.bfloat16)


def attention_bwd(probs, q, k, v, grad):
    heads = q.shape[1] // HEAD_DIM
    head = pl.BlockSpec((BLK, HEAD_DIM), lambda h: (0, h))
    return pl.pallas_call(
        bwd_kernel,
        grid=(heads,),
        in_specs=[pl.BlockSpec((1, BLK, BLK), lambda h: (h, 0, 0)), head, head, head, head],
        out_specs=[head, head, head],
        out_shape=[jax.ShapeDtypeStruct(q.shape, jnp.bfloat16)] * 3,
        compiler_params=params(),
        cost_estimate=pl.CostEstimate(
            flops=heads * 8 * BLK * BLK * HEAD_DIM, bytes_accessed=8 << 20, transcendentals=0
        ),
        name="attention_bwd",
    )(probs, q, k, v, grad)


def pick_kernel(place_ref, o_ref, out_ref):
    out_ref[0] = o_ref[...]


def pick_blocks(place, out_grad):
    return pl.pallas_call(
        pick_kernel,
        grid_spec=pltpu.PrefetchScalarGridSpec(
            num_scalar_prefetch=1,
            grid=(4,),
            in_specs=[pl.BlockSpec((BLK, BLK), lambda i, p: (0, 2 * (4 * p[1] + i) + 1 - p[0]))],
            out_specs=pl.BlockSpec((1, BLK, BLK), lambda i, p: (i, 0, 0)),
        ),
        out_shape=jax.ShapeDtypeStruct((4, BLK, BLK), jnp.bfloat16),
        compiler_params=params(),
        name="pick_blocks",
    )(place, out_grad)


def near(i, p):
    return jnp.minimum(i, 3)


def far(i, p):
    return jnp.maximum(i - 4, 0)


def block_of(i, p):
    return lax.rem(4 * p[1] + i, 8)


def grad_kernel(place_ref, own_ref, near_ref, far_ref, w_ref, scale_ref, out_ref, acc_ref):
    i = pl.program_id(0)
    w = w_ref[...]

    @pl.when(i == 0)
    def _():
        acc_ref[...] = jnp.zeros_like(acc_ref)

    acc_ref[0] += dot(own_ref[...], w, 1, 1)

    @pl.when(i < 4)
    def _():
        acc_ref[1] += dot(near_ref[0], w, 1, 1)

    @pl.when(i >= 4)
    def _():
        acc_ref[1] += dot(far_ref[0], w, 1, 1)

    @pl.when(i == 7)
    def _():
        scale = scale_ref[...]
        x_hi = place_ref[0]
        out_ref[x_hi] = (acc_ref[0] * scale).astype(jnp.bfloat16)
        out_ref[1 - x_hi] = (acc_ref[1] * scale).astype(jnp.bfloat16)


def grad_dot(place, out_grad, near_blocks, far_blocks, weights, scale):
    return pl.pallas_call(
        grad_kernel,
        grid_spec=pltpu.PrefetchScalarGridSpec(
            num_scalar_prefetch=1,
            grid=(8,),
            in_specs=[
                pl.BlockSpec((BLK, BLK), lambda i, p: (0, 2 * block_of(i, p) + p[0])),
                pl.BlockSpec((1, BLK, BLK), lambda i, p: (near(i, p), 0, 0)),
                pl.BlockSpec((1, BLK, BLK), lambda i, p: (far(i, p), 0, 0)),
                pl.BlockSpec((BLK, BLK), lambda i, p: (block_of(i, p), 0)),
                pl.BlockSpec((1, BLK), lambda i, p: (0, 0)),
            ],
            out_specs=pl.BlockSpec((2, BLK, BLK), lambda i, p: (0, 0, 0)),
            scratch_shapes=[pltpu.VMEM((2, BLK, BLK), jnp.float32)],
        ),
        out_shape=jax.ShapeDtypeStruct((2, BLK, BLK), jnp.bfloat16),
        compiler_params=params(),
        cost_estimate=pl.CostEstimate(
            flops=4 * BLK * BLK * BLK * 8, bytes_accessed=13 << 20, transcendentals=0
        ),
        name="grad_dot",
    )(place, out_grad, near_blocks, far_blocks, weights, scale)


def weight_kernel(place_ref, a_ref, b_ref, own_ref, near_ref, far_ref, out_ref, at_ref, bt_ref):
    i = pl.program_id(0)

    @pl.when(i == 0)
    def _():
        at_ref[...] = a_ref[...].T
        bt_ref[...] = b_ref[...].T

    mine = dot(at_ref[...], own_ref[...], 1, 0)

    @pl.when(i < 4)
    def _():
        out_ref[...] = (mine + dot(bt_ref[...], near_ref[0], 1, 0)).astype(jnp.bfloat16)

    @pl.when(i >= 4)
    def _():
        out_ref[...] = (mine + dot(bt_ref[...], far_ref[0], 1, 0)).astype(jnp.bfloat16)


def weight_dot(place, rotated, rotated_other, out_grad, near_blocks, far_blocks):
    whole = pl.BlockSpec((BLK, BLK), lambda i, p: (0, 0))
    return pl.pallas_call(
        weight_kernel,
        grid_spec=pltpu.PrefetchScalarGridSpec(
            num_scalar_prefetch=1,
            grid=(8,),
            in_specs=[
                whole,
                whole,
                pl.BlockSpec((BLK, BLK), lambda i, p: (0, 2 * block_of(i, p) + p[0])),
                pl.BlockSpec((1, BLK, BLK), lambda i, p: (near(i, p), 0, 0)),
                pl.BlockSpec((1, BLK, BLK), lambda i, p: (far(i, p), 0, 0)),
            ],
            out_specs=pl.BlockSpec((BLK, BLK), lambda i, p: (block_of(i, p), 0)),
            scratch_shapes=[pltpu.VMEM((BLK, BLK), jnp.bfloat16)] * 2,
        ),
        out_shape=jax.ShapeDtypeStruct((8 * BLK, BLK), jnp.bfloat16),
        compiler_params=params(),
        cost_estimate=pl.CostEstimate(
            flops=4 * BLK * BLK * BLK * 8, bytes_accessed=13 << 20, transcendentals=0
        ),
        name="weight_dot",
    )(place, rotated, rotated_other, out_grad, near_blocks, far_blocks)


def mix_kernel(parts, x_ref, out_ref):
    x = x_ref[...].astype(jnp.float32)
    rows = x.shape[0] // parts
    total = x[:rows]
    for part in range(1, parts):
        total = total + x[part * rows : (part + 1) * rows]
    tokens = rows // 16
    blocks = [
        [total[s * tokens : (s + 1) * tokens, c * HEAD_DIM : (c + 1) * HEAD_DIM] for c in range(4)]
        for s in range(16)
    ]
    flat = [blocks[s][c] for s in range(16) for c in range(4)]
    step = 1
    while step < 64:
        flat = [
            flat[i] + flat[i + step] if not i & step else flat[i - step] - flat[i]
            for i in range(64)
        ]
        step *= 2
    for s in range(16):
        for c in range(4):
            out_ref[s * tokens : (s + 1) * tokens, c * HEAD_DIM : (c + 1) * HEAD_DIM] = (
                flat[s * 4 + c] * (1.0 / math.sqrt(HEADS))
            ).astype(jnp.bfloat16)


def mix(x, parts):
    return pl.pallas_call(
        functools.partial(mix_kernel, parts),
        out_shape=jax.ShapeDtypeStruct((x.shape[0] // parts, x.shape[1]), jnp.bfloat16),
        compiler_params=params(),
        name="mix",
    )(x)


def body(queries, keys, values, out_grad, o_weight, exponents, valid_lengths):
    x_hi, core = lax.axis_index("xh"), lax.axis_index("co")
    place = jnp.stack([x_hi, core]).astype(jnp.int32)
    scale = jnp.exp2(exponents.astype(jnp.float32))

    weights = lax.all_gather(o_weight, "z", axis=0, tiled=True)
    across = [((h * 2 + l), (1 - h) * 2 + 1 - l) for h in range(2) for l in range(2)]
    near_blocks = lax.ppermute(pick_blocks(place, out_grad), ("xh", "xl"), across)
    far_blocks = lax.ppermute(near_blocks, "co", [(0, 1), (1, 0)])

    attended, probs = attention_fwd(valid_lengths, queries, keys, values)
    turned = lax.all_to_all(attended, TENSOR, 0, 0, tiled=True)
    rotated = lax.all_to_all(mix(turned, 1), TENSOR, 0, 0, tiled=True)
    rotated_other = lax.ppermute(rotated, "xh", [(0, 1), (1, 0)])
    partial = weight_dot(place, rotated, rotated_other, out_grad, near_blocks, far_blocks)
    summed = lax.psum_scatter(partial, "z", scatter_dimension=0, tiled=True)

    grad_rotated = grad_dot(place, out_grad, near_blocks, far_blocks, weights, scale[None, :])
    turned = lax.all_to_all(grad_rotated.reshape(2 * BLK, BLK), ("xh",) + TENSOR, 0, 0, tiled=True)
    grad_attended = lax.all_to_all(mix(turned, 2), TENSOR, 0, 0, tiled=True)
    grad_query, grad_key, grad_value = attention_bwd(probs, queries, keys, values, grad_attended)

    grad_weight = summed.astype(jnp.float32) * scale[:, None]
    return grad_query, grad_key, grad_value, grad_weight


def solution(mesh):
    fine = Mesh(mesh.devices.reshape(8, 2, 4, 2, 2), DP + TENSOR)
    return jax.shard_map(
        body,
        mesh=fine,
        in_specs=(
            P(DP, TENSOR),
            P(DP, TENSOR),
            P(DP, TENSOR),
            P(DP, None),
            P(TENSOR, DP),
            P(TENSOR),
            P(DP),
        ),
        out_specs=(P(DP, TENSOR), P(DP, TENSOR), P(DP, TENSOR), P(TENSOR, DP)),
        check_vma=False,
    )
```

time: 409 us -> 190 us (0.46)
  waiting for transfers between devices: 266 us -> 57.4 us
  matrix products: 46.5 us -> 0 us
  Pallas kernels: 0 us -> 36.8 us
  starting transfers between devices: 0.08 us -> 9.13 us
  local copies, waits for them, and re-layouts: 8.66 us -> 3.61 us
    reduce_scatter x1, waiting for transfers between devices: 162 us -> 1.34 us  [body(): summed = lax.psum_scatter(partial, 'z', scatter_dimension=0, tiled=True)]
    all_gather x1, waiting for transfers between devices: 103 us -> 0.01 us  [body(): weights = lax.all_gather(o_weight, 'z', axis=0, tiled=True)]
    ppermute x0 -> x3, waiting for transfers between devices: none -> 55.4 us  [the longest x1 44.3 us: body(): lax.ppermute(pick_blocks(place, out_grad), ('xh', 'xl'), across)]
    dot_general x9 -> x0, matrix products: 42.8 us -> none  [the longest x1 10.3 us: body(): lax.dot_general(columns, lax.all_gather(o_weight, 'dp', axis=1, tiled=Tru...]
    pallas_call x0 -> x7, Pallas kernels: none -> 36.8 us  [the longest x1 11 us: weight_dot(): pl.pallas_call(weight_kernel, grid_spec=pltpu.PrefetchScalarGridSpec(num_...]
    ppermute x0 -> x3, starting transfers between devices: none -> 9.06 us  [the longest x1 3.39 us: body(): lax.ppermute(pick_blocks(place, out_grad), ('xh', 'xl'), across)]
  transfers between devices with their start and end apart: 2 -> 5, of which waited for: 2 -> 3; matrix products, arithmetic and copies ran while one was open for 13% -> 0% of each run, Pallas kernels for 0% -> 20%
where the time goes in v1:
time: 190 us; the launch traced here: 189 us
  blocking collectives  64.7 us (34%)
  waiting for transfers between devices  57.4 us (30%)
  Pallas kernels  36.8 us (19%)
  between operations  14.8 us (8%)
  starting transfers between devices  9.13 us (5%)
  local copies, waits for them, and re-layouts  3.61 us (2%)
  other arithmetic  2.23 us (1%)
    ppermute x1, waiting for transfers between devices, body(): lax.ppermute(pick_blocks(place, out_grad), ('xh', 'xl'), across)  44.3 us
    all_to_all x1, blocking collectives, body(): lax.all_to_all(grad_rotated.reshape(2 * BLK, BLK), ('xh',) + TENSOR, 0, 0...  23.9 us
    all_to_all x1, blocking collectives, body(): turned = lax.all_to_all(attended, TENSOR, 0, 0, tiled=True)  14.4 us
    all_to_all x1, blocking collectives, body(): rotated = lax.all_to_all(mix(turned, 1), TENSOR, 0, 0, tiled=True)  13.5 us
    all_to_all x1, blocking collectives, body(): grad_attended = lax.all_to_all(mix(turned, 2), TENSOR, 0, 0, tiled=True)  13 us
    ppermute x1, waiting for transfers between devices, body(): rotated_other = lax.ppermute(rotated, 'xh', [(0, 1), (1, 0)])  11.1 us
    pallas_call x1, Pallas kernels, weight_dot(): pl.pallas_call(weight_kernel, grid_spec=pltpu.PrefetchScalarGridSpec(num_...  11 us
    pallas_call x1, Pallas kernels, grad_dot(): pl.pallas_call(grad_kernel, grid_spec=pltpu.PrefetchScalarGridSpec(num_sc...  10.6 us
  transfers between devices with their start and end apart: 5, of which 3 were waited for; matrix products, arithmetic and copies ran while one was open for 0% of the time, Pallas kernels for 20%

profile of v1, /device:TPU:1, one launch (start us, length us, event | category | flops | bytes accessed | tf_op | source)
XLA Modules:
  0.0 188.7 jit_solution(8788578092231485033)
XLA Ops:
  7.2 0.7 all-gather.2.cloned.1.call-update
  7.9 0.0 reduce-scatter.2.cloned.1.call-start
  7.9 0.1 pad_add_fusion.place_ref
  8.0 2.9 %pick_blocks.1 = bf16[4,512,512]{2,1,0:T(8,128)(2,1)S(1)} custom-call(s32[2]{0:T(128)S(1)} %pad_add_fusion.place_ref, bf16[512,8192]{1,0:T(8,128)(2,1)} %own_ref.3), custom_call_target="tpu_custom_call" | custom-call | tf_op jit(solution)/shard_map/pick_blocks/pallas_call | solution.py:96
  11.0 3.4 %collective-permute-start = (bf16[4,512,512]{2,1,0:T(8,128)(2,1)S(1)}, bf16[4,512,512]{2,1,0:T(8,128)(2,1)S(1)}, u32[]{:S(2)}, u32[]{:S(2)}) collective-permute-start(bf16[4,512,512]{2,1,0:T(8,128)(2,1)S(1)} %pick_blocks.1), channel_id=1, source_target_pairs={{0,18},{2,16},{16,2},{18,0},{1,19},{3,17},{17,3},{19,1},{4,22},{6,... | collective-permute-start | bytes 6291464 | tf_op jit(solution)/shard_map/ppermute | solution.py:260
  14.4 44.3 %collective-permute-done.near_ref = bf16[4,512,512]{2,1,0:T(8,128)(2,1)S(1)} collective-permute-done((bf16[4,512,512]{2,1,0:T(8,128)(2,1)S(1)}, bf16[4,512,512]{2,1,0:T(8,128)(2,1)S(1)}, u32[]{:S(2)}, u32[]{:S(2)}) %collective-permute-start) | collective-permute-done | bytes 2097184 | tf_op jit(solution)/shard_map/ppermute | solution.py:260
  58.7 2.3 %collective-permute-start.1 = (bf16[4,512,512]{2,1,0:T(8,128)(2,1)S(1)}, bf16[4,512,512]{2,1,0:T(8,128)(2,1)S(1)}, u32[]{:S(2)}, u32[]{:S(2)}) collective-permute-start(bf16[4,512,512]{2,1,0:T(8,128)(2,1)S(1)} %collective-permute-done.near_ref), channel_id=1, source_target_pairs={{0,1},{1,0},{2,3},{3,2},{4,5},{5,4},{6,7},{7,6},{8,9},{9,8},{10,11... | collective-permute-start | bytes 6291464 | tf_op jit(solution)/shard_map/ppermute | solution.py:261
  61.6 5.0 %attention_fwd.1 = (bf16[512,512]{1,0:T(8,128)(2,1)S(1)}, f32[4,512,512]{2,1,0:T(8,128)}) custom-call(s32[1]{0:T(128)S(6)} %copy.11.len_ref, bf16[512,512]{1,0:T(8,128)(2,1)S(1)} %copy-done.2, bf16[512,512]{1,0:T(8,128)(2,1)S(1)} %copy-done.3, bf16[512,512]{1,0:T(8,128)(2,1)S(1)} %copy-done.4), custom_call_target="tpu_custom_call" | custom-call | flops 536870912 | bytes 8388608 | tf_op jit(solution)/shard_map/attention_fwd/pallas_call | solution.py:43
  66.6 14.4 %all_to_all.44 = bf16[16,32,512]{2,1,0:T(8,128)(2,1)S(1)} all-to-all(bf16[16,32,512]{2,1,0:T(8,128)(2,1)S(1)} %bitcast.19), channel_id=1, replica_groups=mesh['z'=8,'xh'=2,'y'=4,'xl'=2,'co'=2] {'y','xl','co'}, dimensions={0} | all-to-all | bytes 1048576 | tf_op jit(solution)/shard_map/all_to_all | solution.py:264
  81.0 0.5 mix.3
  81.5 13.5 %all_to_all.45 = bf16[16,32,512]{2,1,0:T(8,128)(2,1)S(1)} all-to-all(bf16[16,32,512]{2,1,0:T(8,128)(2,1)S(1)} %bitcast.18), channel_id=1, replica_groups=mesh['z'=8,'xh'=2,'y'=4,'xl'=2,'co'=2] {'y','xl','co'}, dimensions={0} | all-to-all | bytes 1048576 | tf_op jit(solution)/shard_map/all_to_all | solution.py:265
  94.9 3.4 %collective-permute-start.2 = (bf16[512,512]{1,0:T(8,128)(2,1)S(1)}, bf16[512,512]{1,0:T(8,128)(2,1)S(1)}, u32[]{:S(2)}, u32[]{:S(2)}) collective-permute-start(bf16[512,512]{1,0:T(8,128)(2,1)S(1)} %bitcast.13), channel_id=1, source_target_pairs={{0,16},{16,0},{1,17},{17,1},{2,18},{18,2},{3,19},{19,3},{4,20},{20... | collective-permute-start | bytes 1572872 | tf_op jit(solution)/shard_map/ppermute | solution.py:266
  98.3 11.1 %collective-permute-done.2.b_ref = bf16[512,512]{1,0:T(8,128)(2,1)S(1)} collective-permute-done((bf16[512,512]{1,0:T(8,128)(2,1)S(1)}, bf16[512,512]{1,0:T(8,128)(2,1)S(1)}, u32[]{:S(2)}, u32[]{:S(2)}) %collective-permute-start.2) | collective-permute-done | bytes 524320 | tf_op jit(solution)/shard_map/ppermute | solution.py:266
  109.4 11.0 %weight_dot.1 = bf16[4096,512]{1,0:T(8,128)(2,1)} custom-call(s32[2]{0:T(128)S(1)} %pad_add_fusion.place_ref, bf16[512,512]{1,0:T(8,128)(2,1)S(1)} %bitcast.14, bf16[512,512]{1,0:T(8,128)(2,1)S(1)} %collective-permute-done.2.b_ref, bf16[512,8192]{1,0:T(8,128)(2,1)} %own_ref.3, bf16[4,512,512]{2,1,0:T(8,128)(2,1)S(1)} %collective-permute-done.near_ref, ...), custom_call_target="tpu_custom_call" | custom-call | flops 4294967296 | bytes 13631488 | tf_op jit(solution)/shard_map/weight_dot/pallas_call | solution.py:194
  120.5 1.3 copy-done
  121.8 0.7 copy-done.6
  122.5 1.6 copy-done.1
  124.1 10.6 %grad_dot.1 = bf16[2,512,512]{2,1,0:T(8,128)(2,1)S(1)} custom-call(s32[2]{0:T(128)S(1)} %pad_add_fusion.place_ref, bf16[512,8192]{1,0:T(8,128)(2,1)} %own_ref.3, bf16[4,512,512]{2,1,0:T(8,128)(2,1)S(1)} %collective-permute-done.near_ref, bf16[4,512,512]{2,1,0:T(8,128)(2,1)S(1)} %copy-done.1, bf16[4096,512]{1,0:T(8,128)(2,1)} %all-gather.2.cloned.1.call-done.w_ref, ...), custom_call_target="tpu_custom_call" | custom-call | flops 4294967296 | bytes 13631488 | tf_op jit(solution)/shard_map/grad_dot/pallas_call | solution.py:149
  134.7 23.9 %all_to_all.46 = bf16[32,32,512]{2,1,0:T(8,128)(2,1)S(1)} all-to-all(bf16[32,32,512]{2,1,0:T(8,128)(2,1)S(1)} %bitcast.11), channel_id=1, replica_groups=mesh['z'=8,'xh'=2,'y'=4,'xl'=2,'co'=2] {'xh','y','xl','co'}, dimensions={0} | all-to-all | bytes 2097152 | tf_op jit(solution)/shard_map/all_to_all | solution.py:271
  158.6 0.5 mix.2
  159.1 13.0 %all_to_all.47 = bf16[16,32,512]{2,1,0:T(8,128)(2,1)S(1)} all-to-all(bf16[16,32,512]{2,1,0:T(8,128)(2,1)S(1)} %bitcast.16), channel_id=1, replica_groups=mesh['z'=8,'xh'=2,'y'=4,'xl'=2,'co'=2] {'y','xl','co'}, dimensions={0} | all-to-all | bytes 1048576 | tf_op jit(solution)/shard_map/all_to_all | solution.py:272
  172.1 6.2 %attention_bwd.1 = (bf16[512,512]{1,0:T(8,128)(2,1)}, bf16[512,512]{1,0:T(8,128)(2,1)}, bf16[512,512]{1,0:T(8,128)(2,1)}) custom-call(f32[4,512,512]{2,1,0:T(8,128)} %get-tuple-element.9.p_ref, bf16[512,512]{1,0:T(8,128)(2,1)S(1)} %copy-done.2, bf16[512,512]{1,0:T(8,128)(2,1)S(1)} %copy-done.3, bf16[512,512]{1,0:T(8,128)(2,1)S(1)} %copy-done.5, ...), custom_call_target="tpu_custom_call" | custom-call | flops 1073741824 | bytes 8388608 | tf_op jit(solution)/shard_map/attention_bwd/pallas_call | solution.py:77
  178.4 1.3 reduce-scatter.2.cloned.1.call-done
  179.7 2.1 %convert_multiply_fusion = f32[512,512]{1,0:T(8,128)} fusion(bf16[512,512]{1,0:T(8,128)(2,1)} %reduce-scatter.2.cloned.1.call-done, f32[512]{0:T(512)S(1)} %multiply_exponential_fusion), kind=kLoop, calls=%fused_computation | loop fusion | flops 524288 | bytes 1574912 | tf_op jit(solution)/shard_map/mul | solution.py:275
  (16 shorter events, 0.1 us)
Async XLA Ops:
  7.2 115.3 %all-gather.2.cloned.1.call-start = ((), (), s32[]{:S(2)}) async-start(), calls=%async_computation.5 | async-start | bytes 4718592 | tf_op jit(solution)/shard_map/all_gather | solution.py:258
  7.9 171.8 %reduce-scatter.2.cloned.1.call-start = ((), (), s32[]{:S(2)}) async-start(), calls=%async_computation.6 | async-start | bytes 4718592 | tf_op jit(solution)/shard_map/reduce_scatter | solution.py:268
  8.0 53.6 %copy-start.2 = (bf16[512,512]{1,0:T(8,128)(2,1)S(1)}, bf16[512,512]{1,0:T(8,128)(2,1)}, u32[]{:S(2)}) copy-start(bf16[512,512]{1,0:T(8,128)(2,1)} %q_ref.3) | copy-start | bytes 1572868
  8.0 53.6 %copy-start.3 = (bf16[512,512]{1,0:T(8,128)(2,1)S(1)}, bf16[512,512]{1,0:T(8,128)(2,1)}, u32[]{:S(2)}) copy-start(bf16[512,512]{1,0:T(8,128)(2,1)} %k_ref.3) | copy-start | bytes 1572868
  8.0 53.6 %copy-start.4 = (bf16[512,512]{1,0:T(8,128)(2,1)S(1)}, bf16[512,512]{1,0:T(8,128)(2,1)}, u32[]{:S(2)}) copy-start(bf16[512,512]{1,0:T(8,128)(2,1)} %v_ref.3) | copy-start | bytes 1572868
  11.0 47.7 %collective-permute-start = (bf16[4,512,512]{2,1,0:T(8,128)(2,1)S(1)}, bf16[4,512,512]{2,1,0:T(8,128)(2,1)S(1)}, u32[]{:S(2)}, u32[]{:S(2)}) collective-permute-start(bf16[4,512,512]{2,1,0:T(8,128)(2,1)S(1)} %pick_blocks.1), channel_id=1, source_target_pairs={{0,18},{2,16},{16,2},{18,0},{1,19},{3,17},{17,3},{19,1},{4,22},{6,... | collective-permute-start | bytes 6291464 | tf_op jit(solution)/shard_map/ppermute | solution.py:260
  58.7 50.7 %collective-permute-start.1 = (bf16[4,512,512]{2,1,0:T(8,128)(2,1)S(1)}, bf16[4,512,512]{2,1,0:T(8,128)(2,1)S(1)}, u32[]{:S(2)}, u32[]{:S(2)}) collective-permute-start(bf16[4,512,512]{2,1,0:T(8,128)(2,1)S(1)} %collective-permute-done.near_ref), channel_id=1, source_target_pairs={{0,1},{1,0},{2,3},{3,2},{4,5},{5,4},{6,7},{7,6},{8,9},{9,8},{10,11... | collective-permute-start | bytes 6291464 | tf_op jit(solution)/shard_map/ppermute | solution.py:261
  94.9 14.5 %collective-permute-start.2 = (bf16[512,512]{1,0:T(8,128)(2,1)S(1)}, bf16[512,512]{1,0:T(8,128)(2,1)S(1)}, u32[]{:S(2)}, u32[]{:S(2)}) collective-permute-start(bf16[512,512]{1,0:T(8,128)(2,1)S(1)} %bitcast.13), channel_id=1, source_target_pairs={{0,16},{16,0},{1,17},{17,1},{2,18},{18,2},{3,19},{19,3},{4,20},{20... | collective-permute-start | bytes 1572872 | tf_op jit(solution)/shard_map/ppermute | solution.py:266
  120.5 1.3 copy-start
  121.8 0.7 copy-start.6
  122.5 1.6 copy-start.1
  134.7 37.4 %copy-start.5 = (bf16[512,512]{1,0:T(8,128)(2,1)S(1)}, bf16[512,512]{1,0:T(8,128)(2,1)}, u32[]{:S(2)}) copy-start(bf16[512,512]{1,0:T(8,128)(2,1)} %v_ref.3) | copy-start | bytes 1572868
Sparse Core Ops, SparseCore 0:
  9.8 58.6 all-gather.1
  121.9 57.7 reduce-scatter.1

commit v2 on v1

v2 whole, which is shorter than its diff:
```python
import functools
import math

import jax
import jax.numpy as jnp
from jax import lax
from jax.experimental import pallas as pl
from jax.experimental.pallas import tpu as pltpu
from jax.sharding import Mesh
from jax.sharding import PartitionSpec as P

HEADS = 64
HEAD_DIM = 128
DP = ("z", "xh")
TENSOR = ("y", "xl", "co")
BLK = 512


def params(mib=60):
    return pltpu.CompilerParams(vmem_limit_bytes=mib * 1024 * 1024)


def dot(a, b, ca, cb):
    return lax.dot_general(a, b, (((ca,), (cb,)), ((), ())), preferred_element_type=jnp.float32)


def fwd_kernel(len_ref, q_ref, k_ref, v_ref, att_ref, p_ref):
    scores = dot(q_ref[...], k_ref[...], 1, 1) * (1.0 / math.sqrt(HEAD_DIM))
    t = lax.broadcasted_iota(jnp.int32, scores.shape, 0)
    s = lax.broadcasted_iota(jnp.int32, scores.shape, 1)
    scores = jnp.where((s <= t) & (s < len_ref[0]), scores, -1e30)
    top = jnp.max(scores, axis=-1, keepdims=True)
    weights = jnp.exp(scores - top)
    probs = weights / jnp.sum(weights, axis=-1, keepdims=True)
    p_ref[0] = probs
    att_ref[...] = dot(probs.astype(jnp.bfloat16), v_ref[...], 1, 0).astype(jnp.bfloat16)


def attention_fwd(length, q, k, v):
    heads = q.shape[1] // HEAD_DIM
    head = pl.BlockSpec((BLK, HEAD_DIM), lambda h, *_: (0, h))
    return pl.pallas_call(
        fwd_kernel,
        grid_spec=pltpu.PrefetchScalarGridSpec(
            num_scalar_prefetch=1,
            grid=(heads,),
            in_specs=[head, head, head],
            out_specs=[head, pl.BlockSpec((1, BLK, BLK), lambda h, *_: (h, 0, 0))],
        ),
        out_shape=[
            jax.ShapeDtypeStruct(q.shape, jnp.bfloat16),
            jax.ShapeDtypeStruct((heads, BLK, BLK), jnp.float32),
        ],
        compiler_params=params(),
        cost_estimate=pl.CostEstimate(
            flops=heads * 4 * BLK * BLK * HEAD_DIM, bytes_accessed=8 << 20, transcendentals=heads * BLK * BLK
        ),
        name="attention_fwd",
    )(length, q, k, v)


def bwd_kernel(p_ref, q_ref, k_ref, v_ref, g_ref, dq_ref, dk_ref, dv_ref):
    probs = p_ref[0]
    grad = g_ref[...]
    dv_ref[...] = dot(probs.astype(jnp.bfloat16), grad, 0, 0).astype(jnp.bfloat16)
    grad_probs = dot(grad, v_ref[...], 1, 1)
    centre = jnp.sum(probs * grad_probs, axis=-1, keepdims=True)
    grad_scores = (probs * (grad_probs - centre) * (1.0 / math.sqrt(HEAD_DIM))).astype(jnp.bfloat16)
    dq_ref[...] = dot(grad_scores, k_ref[...], 1, 0).astype(jnp.bfloat16)
    dk_ref[...] = dot(grad_scores, q_ref[...], 0, 0).astype(jnp.bfloat16)


def attention_bwd(probs, q, k, v, grad):
    heads = q.shape[1] // HEAD_DIM
    head = pl.BlockSpec((BLK, HEAD_DIM), lambda h: (0, h))
    return pl.pallas_call(
        bwd_kernel,
        grid=(heads,),
        in_specs=[pl.BlockSpec((1, BLK, BLK), lambda h: (h, 0, 0)), head, head, head, head],
        out_specs=[head, head, head],
        out_shape=[jax.ShapeDtypeStruct(q.shape, jnp.bfloat16)] * 3,
        compiler_params=params(),
        cost_estimate=pl.CostEstimate(
            flops=heads * 8 * BLK * BLK * HEAD_DIM, bytes_accessed=8 << 20, transcendentals=0
        ),
        name="attention_bwd",
    )(probs, q, k, v, grad)


PIECES = ((0, 3), (3, 3), (6, 1), (7, 1))


def block_of(i, p):
    core = jnp.where((i < 3) | (i == 6), p[1], 1 - p[1])
    return 4 * core + jnp.where(i < 6, p[2] + lax.rem(i, 3), 3 * (1 - p[2]))


ANY = pl.BlockSpec(memory_space=pl.ANY)
SMEM = pl.BlockSpec(memory_space=pltpu.SMEM)
VMEM = pl.BlockSpec(memory_space=pltpu.VMEM)


def place_of(place_ref):
    return place_ref[0], place_ref[1], place_ref[2]


def own_copy(grad_ref, place, buf, sems):
    def copy(i):
        column = pl.multiple_of((2 * block_of(i, place) + place[0]) * BLK, BLK)
        return pltpu.make_async_copy(grad_ref.at[:, pl.ds(column, BLK)], buf.at[i], sems.at[i])

    return copy


def row_copy(ref, buf, sems, index=lambda i: i, out=False):
    def copy(i):
        rows = ref.at[pl.ds(pl.multiple_of(index(i) * BLK, BLK), BLK)]
        if out:
            return pltpu.make_async_copy(buf.at[i], rows, sems.at[i])
        return pltpu.make_async_copy(rows, buf.at[i], sems.at[i])

    return copy


def piece_copies(refs, buf, sems):
    return [
        pltpu.make_async_copy(ref, buf.at[pl.ds(first, count)], sems.at[at])
        for at, (ref, (first, count)) in enumerate(zip(refs, PIECES))
    ]


def each(first, count, step):
    def body(i, carry):
        step(i)
        return carry

    lax.fori_loop(first, first + count, body, 0)


def grad_kernel(place_ref, grad_ref, near, far, last, far_last, w_ref, scale_ref, out_ref, *scratch):
    own_buf, w_buf, piece_buf, acc_ref, own_sems, w_sems, piece_sems = scratch
    place = place_of(place_ref)
    own = own_copy(grad_ref, place, own_buf, own_sems)
    weight = row_copy(w_ref, w_buf, w_sems, lambda i: block_of(i, place))
    pieces = piece_copies((near, far, last, far_last), piece_buf, piece_sems)
    own(0).start()
    weight(0).start()
    pieces[0].start()

    def begin(i):
        own(i).start()
        weight(i).start()

    each(1, 7, begin)
    for piece in pieces[1:]:
        piece.start()
    acc_ref[...] = jnp.zeros_like(acc_ref)

    def step(i):
        own(i).wait()
        weight(i).wait()
        w = w_buf[i]
        acc_ref[0] += dot(own_buf[i], w, 1, 1)
        acc_ref[1] += dot(piece_buf[i], w, 1, 1)

    for piece, (first, count) in zip(pieces, PIECES):
        piece.wait()
        each(first, count, step)
    scale = scale_ref[...]
    x_hi = place[0]
    out_ref[x_hi] = (acc_ref[0] * scale).astype(jnp.bfloat16)
    out_ref[1 - x_hi] = (acc_ref[1] * scale).astype(jnp.bfloat16)


def grad_dot(place, out_grad, pieces, weights, scale):
    blocks = pltpu.VMEM((8, BLK, BLK), jnp.bfloat16)
    return pl.pallas_call(
        grad_kernel,
        in_specs=[SMEM, ANY, *[ANY] * 4, ANY, VMEM],
        out_specs=VMEM,
        scratch_shapes=[
            blocks,
            blocks,
            blocks,
            pltpu.VMEM((2, BLK, BLK), jnp.float32),
            pltpu.SemaphoreType.DMA((8,)),
            pltpu.SemaphoreType.DMA((8,)),
            pltpu.SemaphoreType.DMA((4,)),
        ],
        out_shape=jax.ShapeDtypeStruct((2, BLK, BLK), jnp.bfloat16),
        compiler_params=params(60),
        cost_estimate=pl.CostEstimate(
            flops=4 * BLK * BLK * BLK * 8, bytes_accessed=13 << 20, transcendentals=0
        ),
        name="grad_dot",
    )(place, out_grad, *pieces, weights, scale)


def own_kernel(place_ref, a_ref, grad_ref, out_ref, at_ref, in_buf, out_buf, in_sems, out_sems):
    place = place_of(place_ref)
    own = own_copy(grad_ref, place, in_buf, in_sems)
    out = row_copy(out_ref, out_buf, out_sems, out=True)
    each(0, 8, lambda i: own(i).start())
    at_ref[...] = a_ref[...].T

    def step(i):
        own(i).wait()
        out_buf[i] = dot(at_ref[...], in_buf[i], 1, 0).astype(jnp.bfloat16)
        out(i).start()

    each(0, 8, step)
    each(0, 8, lambda i: out(i).wait())


def own_dot(place, rotated, out_grad):
    blocks = pltpu.VMEM((8, BLK, BLK), jnp.bfloat16)
    return pl.pallas_call(
        own_kernel,
        in_specs=[SMEM, VMEM, ANY],
        out_specs=ANY,
        scratch_shapes=[
            pltpu.VMEM((BLK, BLK), jnp.bfloat16),
            blocks,
            blocks,
            pltpu.SemaphoreType.DMA((8,)),
            pltpu.SemaphoreType.DMA((8,)),
        ],
        out_shape=jax.ShapeDtypeStruct((8 * BLK, BLK), jnp.bfloat16),
        compiler_params=params(60),
        cost_estimate=pl.CostEstimate(
            flops=2 * BLK * BLK * BLK * 8, bytes_accessed=9 << 20, transcendentals=0
        ),
        name="own_dot",
    )(place, rotated, out_grad)


def other_kernel(place_ref, a_ref, own_ref, near, far, last, far_last, out_ref, *scratch):
    at_ref, own_buf, piece_buf, out_buf, own_sems, piece_sems, out_sems = scratch
    place = place_of(place_ref)
    own = row_copy(own_ref, own_buf, own_sems)
    pieces = piece_copies((near, far, last, far_last), piece_buf, piece_sems)
    out = row_copy(out_ref, out_buf, out_sems, lambda i: block_of(i, place), out=True)
    pieces[0].start()
    each(0, 8, lambda i: own(i).start())
    for piece in pieces[1:]:
        piece.start()
    at_ref[...] = a_ref[...].T

    def step(i):
        own(i).wait()
        total = own_buf[i].astype(jnp.float32) + dot(at_ref[...], piece_buf[i], 1, 0)
        out_buf[i] = total.astype(jnp.bfloat16)
        out(i).start()

    for piece, (first, count) in zip(pieces, PIECES):
        piece.wait()
        each(first, count, step)
    each(0, 8, lambda i: out(i).wait())


def other_dot(place, rotated, own, pieces):
    blocks = pltpu.VMEM((8, BLK, BLK), jnp.bfloat16)
    return pl.pallas_call(
        other_kernel,
        in_specs=[SMEM, VMEM, ANY, *[ANY] * 4],
        out_specs=ANY,
        scratch_shapes=[
            pltpu.VMEM((BLK, BLK), jnp.bfloat16),
            blocks,
            blocks,
            blocks,
            pltpu.SemaphoreType.DMA((8,)),
            pltpu.SemaphoreType.DMA((4,)),
            pltpu.SemaphoreType.DMA((8,)),
        ],
        out_shape=jax.ShapeDtypeStruct((8 * BLK, BLK), jnp.bfloat16),
        compiler_params=params(60),
        cost_estimate=pl.CostEstimate(
            flops=2 * BLK * BLK * BLK * 8, bytes_accessed=13 << 20, transcendentals=0
        ),
        name="other_dot",
    )(place, rotated, own, *pieces)


def mix_kernel(parts, copies, x_ref, out_ref):
    x = x_ref[...].astype(jnp.float32)
    rows = x.shape[0] // parts
    total = x[:rows]
    for part in range(1, parts):
        total = total + x[part * rows : (part + 1) * rows]
    tokens = rows // 16
    blocks = [
        [total[s * tokens : (s + 1) * tokens, c * HEAD_DIM : (c + 1) * HEAD_DIM] for c in range(4)]
        for s in range(16)
    ]
    flat = [blocks[s][c] for s in range(16) for c in range(4)]
    step = 1
    while step < 64:
        flat = [
            flat[i] + flat[i + step] if not i & step else flat[i - step] - flat[i]
            for i in range(64)
        ]
        step *= 2
    for s in range(16):
        for c in range(4):
            mixed = (flat[s * 4 + c] * (1.0 / math.sqrt(HEADS))).astype(jnp.bfloat16)
            for copy in range(copies):
                first = copy * rows + s * tokens
                out_ref[first : first + tokens, c * HEAD_DIM : (c + 1) * HEAD_DIM] = mixed


def mix(x, parts, copies):
    return pl.pallas_call(
        functools.partial(mix_kernel, parts, copies),
        out_shape=jax.ShapeDtypeStruct((x.shape[0] // parts * copies, x.shape[1]), jnp.bfloat16),
        compiler_params=params(16),
        name="mix",
    )(x)


def body(queries, keys, values, out_grad, o_weight, exponents, valid_lengths):
    x_hi, core, y = (lax.axis_index(name) for name in ("xh", "co", "y"))
    y_bit = lax.rem(y, 2)
    place = jnp.stack([x_hi, core, y_bit]).astype(jnp.int32)
    scale = jnp.exp2(exponents.astype(jnp.float32))

    weights = lax.all_gather(o_weight, "z", axis=0, tiled=True)

    across = [(h * 2 + l, (1 - h) * 2 + 1 - l) for h in range(2) for l in range(2)]
    swap, pairs = [(0, 1), (1, 0)], [(0, 1), (1, 0), (2, 3), (3, 2)]
    picked = jnp.stack(
        [
            lax.dynamic_slice(out_grad, (0, (2 * (4 * core + y_bit + i) + 1 - x_hi) * BLK), (BLK, BLK))
            for i in range(3)
        ]
    )
    near = lax.ppermute(picked, ("xh", "xl"), across)

    queries, _ = lax.optimization_barrier((queries, picked))
    attended, probs = attention_fwd(valid_lengths, queries, keys, values)
    turned = lax.all_to_all(attended, TENSOR, 0, 0, tiled=True)
    rotated = lax.all_to_all(mix(turned, 1, 1), TENSOR, 0, 0, tiled=True)
    rotated_other = lax.ppermute(rotated, "xh", swap)
    near, rotated = lax.optimization_barrier((near, rotated))
    last = lax.ppermute(lax.dynamic_slice(near, (2 * y_bit, 0, 0), (1, BLK, BLK)), "y", pairs)
    far = lax.ppermute(near, "co", swap)
    own = own_dot(place, rotated, out_grad)
    last, own = lax.optimization_barrier((last, own))
    far_last = lax.ppermute(last, "co", swap)
    pieces = [near, far, last, far_last]
    partial = other_dot(place, rotated_other, own, pieces)
    summed = lax.psum_scatter(partial, "z", scatter_dimension=0, tiled=True)

    grad_rotated = grad_dot(place, out_grad, pieces, weights, scale[None, :])
    turned = lax.all_to_all(grad_rotated.reshape(2 * BLK, BLK), ("xh",) + TENSOR, 0, 0, tiled=True)
    grad_attended = lax.all_to_all(mix(turned, 2, 1), TENSOR, 0, 0, tiled=True)
    grad_query, grad_key, grad_value = attention_bwd(probs, queries, keys, values, grad_attended)

    grad_weight = summed.astype(jnp.float32) * scale[:, None]
    return grad_query, grad_key, grad_value, grad_weight


def solution(mesh):
    fine = Mesh(mesh.devices.reshape(8, 2, 4, 2, 2), DP + TENSOR)
    return jax.shard_map(
        body,
        mesh=fine,
        in_specs=(
            P(DP, TENSOR),
            P(DP, TENSOR),
            P(DP, TENSOR),
            P(DP, None),
            P(TENSOR, DP),
            P(TENSOR),
            P(DP),
        ),
        out_specs=(P(DP, TENSOR), P(DP, TENSOR), P(DP, TENSOR), P(TENSOR, DP)),
        check_vma=False,
    )
```

time: 190 us -> 144 us (0.76)
  waiting for transfers between devices: 57.4 us -> 10.1 us
  starting transfers between devices: 9.13 us -> 6.5 us
    ppermute x3 -> x5, waiting for transfers between devices: 55.4 us -> 6.98 us  [the longest x1 5.44 us: body(): lax.ppermute(lax.dynamic_slice(near, (2 * y_bit, 0, 0), (1, BLK, BLK)), '...]
    ppermute x3 -> x5, starting transfers between devices: 9.06 us -> 6.42 us  [the longest x1 3.39 us: body(): near = lax.ppermute(picked, ('xh', 'xl'), across)]
  transfers between devices with their start and end apart: 5 -> 7, of which waited for: 3 -> 4; matrix products, arithmetic and copies ran while one was open for 0% -> 3% of each run, Pallas kernels for 20% -> 26%
where the time goes in v2:
time: 144 us; the launch traced here: 143 us
  blocking collectives  66.1 us (46%)
  Pallas kernels  37.4 us (26%)
  between operations  14.8 us (10%)
  waiting for transfers between devices  10.1 us (7%)
  starting transfers between devices  6.5 us (5%)
  local copies, waits for them, and re-layouts  4.9 us (3%)
  other arithmetic  3.53 us (2%)
    all_to_all x1, blocking collectives, body(): lax.all_to_all(grad_rotated.reshape(2 * BLK, BLK), ('xh',) + TENSOR, 0, 0...  23.4 us
    all_to_all x1, blocking collectives, body(): turned = lax.all_to_all(attended, TENSOR, 0, 0, tiled=True)  15.3 us
    all_to_all x1, blocking collectives, body(): rotated = lax.all_to_all(mix(turned, 1, 1), TENSOR, 0, 0, tiled=True)  14.1 us
    all_to_all x1, blocking collectives, body(): grad_attended = lax.all_to_all(mix(turned, 2, 1), TENSOR, 0, 0, tiled=True)  13.4 us
    pallas_call x1, Pallas kernels, grad_dot(): pl.pallas_call(grad_kernel, in_specs=[SMEM, ANY, *[ANY] * 4, ANY, VMEM],...  9.85 us
    pallas_call x1, Pallas kernels, other_dot(): pl.pallas_call(other_kernel, in_specs=[SMEM, VMEM, ANY, *[ANY] * 4], out_...  7.6 us
    pallas_call x1, Pallas kernels, own_dot(): pl.pallas_call(own_kernel, in_specs=[SMEM, VMEM, ANY], out_specs=ANY, scr...  6.62 us
    pallas_call x1, Pallas kernels, attention_bwd(): pl.pallas_call(bwd_kernel, grid=(heads,), in_specs=[pl.BlockSpec((1, BLK,...  6.54 us
  transfers between devices with their start and end apart: 7, of which 4 were waited for; matrix products, arithmetic and copies ran while one was open for 3% of the time, Pallas kernels for 26%

profile of v2, /device:TPU:1, one launch (start us, length us, event | category | flops | bytes accessed | tf_op | source)
XLA Modules:
  0.0 143.3 jit_solution(17218175026066143405)
XLA Ops:
  7.2 0.7 all-gather.2.cloned.1.call-update
  8.0 1.5 %dynamic-slice_bitcast_fusion.2 = (bf16[1,512,512]{2,1,0:T(8,128)(2,1)S(1)}, bf16[1,512,512]{2,1,0:T(8,128)(2,1)S(1)}, bf16[1,512,512]{2,1,0:T(8,128)(2,1)S(1)}) fusion(bf16[512,8192]{1,0:T(8,128)(2,1)} %grad_ref.3, s32[]{:T(128)S(6)} %select_n.12, s32[]{:T(128)S(6)} %select_n.14, s32[]{:T(128)S(6)} %select_n.13), kind=kLoop, calls=%fused_computation.4 | loop fusion | bytes 3145740 | tf_op jit(solution)/shard_map/stack | solution.py:331
  9.6 3.4 %collective-permute-start = (bf16[3,512,512]{2,1,0:T(8,128)(2,1)S(1)}, bf16[3,512,512]{2,1,0:T(8,128)(2,1)S(1)}, u32[]{:S(2)}, u32[]{:S(2)}) collective-permute-start(bf16[3,512,512]{2,1,0:T(8,128)(2,1)S(1)} %pad_maximum_fusion), channel_id=1, source_target_pairs={{0,18},{2,16},{16,2},{18,0},{1,19},{3,17},{17,3},{19,1},{4,22},{6,... | collective-permute-start | bytes 4718600 | tf_op jit(solution)/shard_map/ppermute | solution.py:337
  13.7 5.8 %attention_fwd.1 = (bf16[512,512]{1,0:T(8,128)(2,1)}, f32[4,512,512]{2,1,0:T(8,128)}) custom-call(s32[1]{0:T(128)S(6)} %copy.11.len_ref, bf16[512,512]{1,0:T(8,128)(2,1)} %q_ref.1, bf16[512,512]{1,0:T(8,128)(2,1)} %k_ref.3, bf16[512,512]{1,0:T(8,128)(2,1)} %v_ref.3), custom_call_target="tpu_custom_call" | custom-call | flops 536870912 | bytes 8388608 | tf_op jit(solution)/shard_map/attention_fwd/pallas_call | solution.py:42
  19.4 15.3 %all_to_all.45 = bf16[16,32,512]{2,1,0:T(8,128)(2,1)S(1)} all-to-all(bf16[16,32,512]{2,1,0:T(8,128)(2,1)} %bitcast.26), channel_id=1, replica_groups=mesh['z'=8,'xh'=2,'y'=4,'xl'=2,'co'=2] {'y','xl','co'}, dimensions={0} | all-to-all | bytes 1048576 | tf_op jit(solution)/shard_map/all_to_all | solution.py:341
  35.2 14.1 %all_to_all.46 = bf16[16,32,512]{2,1,0:T(8,128)(2,1)} all-to-all(bf16[16,32,512]{2,1,0:T(8,128)(2,1)S(1)} %bitcast.21), channel_id=1, replica_groups=mesh['z'=8,'xh'=2,'y'=4,'xl'=2,'co'=2] {'y','xl','co'}, dimensions={0} | all-to-all | bytes 1048576 | tf_op jit(solution)/shard_map/all_to_all | solution.py:342
  49.3 1.2 collective-permute-start.1
  50.4 0.8 constant_dynamic-slice_fusion
  51.3 0.6 pad_add_fusion.place_ref
  51.9 1.1 collective-permute-start.4
  53.0 6.6 %own_dot.1.own_ref = bf16[4096,512]{1,0:T(8,128)(2,1)} custom-call(s32[3]{0:T(128)} %pad_add_fusion.place_ref, bf16[512,512]{1,0:T(8,128)(2,1)} %bitcast.24, bf16[512,8192]{1,0:T(8,128)(2,1)} %grad_ref.3), custom_call_target="tpu_custom_call" | custom-call | flops 2147483648 | bytes 9437184 | tf_op jit(solution)/shard_map/own_dot/pallas_call | solution.py:217
  59.6 5.4 %collective-permute-done.2.last = bf16[1,512,512]{2,1,0:T(8,128)(2,1)S(1)} collective-permute-done((bf16[1,512,512]{2,1,0:T(8,128)(2,1)}, bf16[1,512,512]{2,1,0:T(8,128)(2,1)S(1)}, u32[]{:S(2)}, u32[]{:S(2)}) %collective-permute-start.2) | collective-permute-done | bytes 524320 | tf_op jit(solution)/shard_map/ppermute | solution.py:345
  65.1 0.8 collective-permute-start.3
  65.8 1.4 collective-permute-done.4.a_ref
  67.4 0.8 copy-done.3
  68.2 1.1 copy-done.1
  69.3 7.6 %other_dot.1 = bf16[4096,512]{1,0:T(8,128)(2,1)} custom-call(s32[3]{0:T(128)} %pad_add_fusion.place_ref, bf16[512,512]{1,0:T(8,128)(2,1)} %collective-permute-done.4.a_ref, bf16[4096,512]{1,0:T(8,128)(2,1)} %own_dot.1.own_ref, bf16[3,512,512]{2,1,0:T(8,128)(2,1)} %copy-done, bf16[3,512,512]{2,1,0:T(8,128)(2,1)} %copy-done.1, bf16[1,512,512]{2,1,0:T(8,128)(2,1)} %copy-done.2, ...), custom_call_target="tpu_custom_call" | custom-call | flops 2147483648 | bytes 13631488 | tf_op jit(solution)/shard_map/other_dot/pallas_call | solution.py:263
  77.0 0.6 copy-done.5
  78.2 9.9 %grad_dot.1 = bf16[2,512,512]{2,1,0:T(8,128)(2,1)} custom-call(s32[3]{0:T(128)} %pad_add_fusion.place_ref, bf16[512,8192]{1,0:T(8,128)(2,1)} %grad_ref.3, bf16[3,512,512]{2,1,0:T(8,128)(2,1)} %copy-done, bf16[3,512,512]{2,1,0:T(8,128)(2,1)} %copy-done.1, bf16[1,512,512]{2,1,0:T(8,128)(2,1)} %copy-done.2, bf16[1,512,512]{2,1,0:T(8,128)(2,1)} %copy-done.3, ...), custom_call_target="tpu_custom_call" | custom-call | flops 4294967296 | bytes 13631488 | tf_op jit(solution)/shard_map/grad_dot/pallas_call | solution.py:177
  88.1 23.4 %all_to_all.47 = bf16[32,32,512]{2,1,0:T(8,128)(2,1)S(1)} all-to-all(bf16[32,32,512]{2,1,0:T(8,128)(2,1)} %bitcast.22), channel_id=1, replica_groups=mesh['z'=8,'xh'=2,'y'=4,'xl'=2,'co'=2] {'xh','y','xl','co'}, dimensions={0} | all-to-all | bytes 2097152 | tf_op jit(solution)/shard_map/all_to_all | solution.py:355
  112.0 13.4 %all_to_all.48 = bf16[16,32,512]{2,1,0:T(8,128)(2,1)} all-to-all(bf16[16,32,512]{2,1,0:T(8,128)(2,1)S(1)} %bitcast.19), channel_id=1, replica_groups=mesh['z'=8,'xh'=2,'y'=4,'xl'=2,'co'=2] {'y','xl','co'}, dimensions={0} | all-to-all | bytes 1048576 | tf_op jit(solution)/shard_map/all_to_all | solution.py:356
  125.3 6.5 %attention_bwd.1 = (bf16[512,512]{1,0:T(8,128)(2,1)}, bf16[512,512]{1,0:T(8,128)(2,1)}, bf16[512,512]{1,0:T(8,128)(2,1)}) custom-call(f32[4,512,512]{2,1,0:T(8,128)} %get-tuple-element.15.p_ref, bf16[512,512]{1,0:T(8,128)(2,1)} %q_ref.1, bf16[512,512]{1,0:T(8,128)(2,1)} %k_ref.3, bf16[512,512]{1,0:T(8,128)(2,1)} %v_ref.3, bf16[512,512]{1,0:T(8,128)(2,1)} %bitcast.25), custom_call_target="tpu_custom_call" | custom-call | flops 1073741824 | bytes 8388608 | tf_op jit(solution)/shard_map/attention_bwd/pallas_call | solution.py:76
  131.9 2.4 %reduce-scatter.2.cloned.1.call-done = bf16[512,512]{1,0:T(8,128)(2,1)} async-done(((bf16[4096,512]{1,0:T(8,128)(2,1)}), bf16[512,512]{1,0:T(8,128)(2,1)}) %reduce-scatter.2.cloned.1.call-update) | async-done | bytes 524304 | tf_op jit(solution)/shard_map/reduce_scatter | solution.py:352
  134.3 2.1 %convert_multiply_fusion = f32[512,512]{1,0:T(8,128)} fusion(bf16[512,512]{1,0:T(8,128)(2,1)} %reduce-scatter.2.cloned.1.call-done, f32[512]{0:T(512)S(1)} %copy-done.4), kind=kLoop, calls=%fused_computation.1 | loop fusion | flops 524288 | bytes 1574912 | tf_op jit(solution)/shard_map/mul | solution.py:359
  (21 shorter events, 2.0 us)
Async XLA Ops:
  7.2 71.0 %all-gather.2.cloned.1.call-start = ((), (), s32[]{:S(2)}) async-start(), calls=%async_computation.5 | async-start | bytes 4718592 | tf_op jit(solution)/shard_map/all_gather | solution.py:327
  7.9 126.4 %reduce-scatter.2.cloned.1.call-start = ((), (), s32[]{:S(2)}) async-start(), calls=%async_computation.6 | async-start | bytes 4718592 | tf_op jit(solution)/shard_map/reduce_scatter | solution.py:352
  9.6 39.6 %collective-permute-start = (bf16[3,512,512]{2,1,0:T(8,128)(2,1)S(1)}, bf16[3,512,512]{2,1,0:T(8,128)(2,1)S(1)}, u32[]{:S(2)}, u32[]{:S(2)}) collective-permute-start(bf16[3,512,512]{2,1,0:T(8,128)(2,1)S(1)} %pad_maximum_fusion), channel_id=1, source_target_pairs={{0,18},{2,16},{16,2},{18,0},{1,19},{3,17},{17,3},{19,1},{4,22},{6,... | collective-permute-start | bytes 4718600 | tf_op jit(solution)/shard_map/ppermute | solution.py:337
  49.3 10.3 %copy-start = (bf16[3,512,512]{2,1,0:T(8,128)(2,1)}, bf16[3,512,512]{2,1,0:T(8,128)(2,1)S(1)}, u32[]{:S(2)}) copy-start(bf16[3,512,512]{2,1,0:T(8,128)(2,1)S(1)} %collective-permute-done.near) | copy-start | bytes 4718596
  49.3 18.9 %collective-permute-start.1 = (bf16[3,512,512]{2,1,0:T(8,128)(2,1)S(1)}, bf16[3,512,512]{2,1,0:T(8,128)(2,1)S(1)}, u32[]{:S(2)}, u32[]{:S(2)}) collective-permute-start(bf16[3,512,512]{2,1,0:T(8,128)(2,1)S(1)} %collective-permute-done.near), channel_id=1, source_target_pairs={{0,1},{1,0},{2,3},{3,2},{4,5},{5,4},{6,7},{7,6},{8,9},{9,8},{10,11... | collective-permute-start | bytes 4718600 | tf_op jit(solution)/shard_map/ppermute | solution.py:346
  51.3 13.8 %collective-permute-start.2 = (bf16[1,512,512]{2,1,0:T(8,128)(2,1)}, bf16[1,512,512]{2,1,0:T(8,128)(2,1)S(1)}, u32[]{:S(2)}, u32[]{:S(2)}) collective-permute-start(bf16[1,512,512]{2,1,0:T(8,128)(2,1)} %constant_dynamic-slice_fusion), channel_id=1, source_target_pairs={{0,4},{4,0},{8,12},{12,8},{1,5},{5,1},{9,13},{13,9},{2,6},{6,2},{1... | collective-permute-start | bytes 1572872 | tf_op jit(solution)/shard_map/ppermute | solution.py:345
  51.9 15.3 %collective-permute-start.4 = (bf16[512,512]{1,0:T(8,128)(2,1)}, bf16[512,512]{1,0:T(8,128)(2,1)}, u32[]{:S(2)}, u32[]{:S(2)}) collective-permute-start(bf16[512,512]{1,0:T(8,128)(2,1)} %bitcast.23), channel_id=1, source_target_pairs={{0,16},{16,0},{1,17},{17,1},{2,18},{18,2},{3,19},{19,3},{4,20},{20... | collective-permute-start | bytes 1572872 | tf_op jit(solution)/shard_map/ppermute | solution.py:343
  65.1 3.1 %copy-start.2 = (bf16[1,512,512]{2,1,0:T(8,128)(2,1)}, bf16[1,512,512]{2,1,0:T(8,128)(2,1)S(1)}, u32[]{:S(2)}) copy-start(bf16[1,512,512]{2,1,0:T(8,128)(2,1)S(1)} %collective-permute-done.2.last) | copy-start | bytes 1572868
  65.1 2.3 %collective-permute-start.3 = (bf16[1,512,512]{2,1,0:T(8,128)(2,1)S(1)}, bf16[1,512,512]{2,1,0:T(8,128)(2,1)S(1)}, u32[]{:S(2)}, u32[]{:S(2)}) collective-permute-start(bf16[1,512,512]{2,1,0:T(8,128)(2,1)S(1)} %collective-permute-done.2.last), channel_id=1, source_target_pairs={{0,1},{1,0},{2,3},{3,2},{4,5},{5,4},{6,7},{7,6},{8,9},{9,8},{10,11... | collective-permute-start | bytes 1572872 | tf_op jit(solution)/shard_map/ppermute | solution.py:349
  67.4 0.8 copy-start.3
  68.2 1.1 copy-start.1
  76.9 0.7 copy-start.5
  125.3 9.0 %copy-start.4 = (f32[512]{0:T(512)S(1)}, f32[512]{0:T(512)}, u32[]{:S(2)}) copy-start(f32[512]{0:T(512)} %multiply_exponential_fusion) | copy-start | bytes 6148
Sparse Core Ops, SparseCore 0:
  9.8 58.6 all-gather.1
  77.1 57.1 reduce-scatter.1

commit v3 on v2

v3 whole, which is shorter than its diff:
```python
import functools
import math

import jax
import jax.numpy as jnp
from jax import lax
from jax.experimental import pallas as pl
from jax.experimental.pallas import tpu as pltpu
from jax.sharding import Mesh
from jax.sharding import PartitionSpec as P

HEADS = 64
HEAD_DIM = 128
DP = ("z", "xh")
TENSOR = ("y", "xl", "co")
BLK = 512


ANY = pl.BlockSpec(memory_space=pl.ANY)
HBM = pl.BlockSpec(memory_space=pltpu.HBM)
SMEM = pl.BlockSpec(memory_space=pltpu.SMEM)
VMEM = pl.BlockSpec(memory_space=pltpu.VMEM)
FWD, BWD = 24, 24
OVER_X = 6
OVER_Y = 8 - OVER_X


def params(mib=60):
    return pltpu.CompilerParams(vmem_limit_bytes=mib * 1024 * 1024)


def dot(a, b, ca, cb):
    return lax.dot_general(a, b, (((ca,), (cb,)), ((), ())), preferred_element_type=jnp.float32)


HALF = BLK // 2


def fwd_kernel(len_ref, q_ref, k_ref, v_ref, att_ref, p_ref):
    for head in range(p_ref.shape[0]):
        cols = slice(head * HEAD_DIM, (head + 1) * HEAD_DIM)
        for first, keys in ((0, HALF), (HALF, BLK)):
            rows = slice(first, first + HALF)
            scores = dot(q_ref[rows, cols], k_ref[:keys, cols], 1, 1) * (1.0 / math.sqrt(HEAD_DIM))
            t = first + lax.broadcasted_iota(jnp.int32, scores.shape, 0)
            s = lax.broadcasted_iota(jnp.int32, scores.shape, 1)
            scores = jnp.where(s < jnp.minimum(t + 1, len_ref[0]), scores, -1e30)
            top = jnp.max(scores, axis=-1, keepdims=True)
            weights = jnp.exp(scores - top)
            probs = (weights * (1.0 / jnp.sum(weights, axis=-1, keepdims=True))).astype(jnp.bfloat16)
            p_ref[head, rows, :keys] = probs
            att_ref[rows, cols] = dot(probs, v_ref[:keys, cols], 1, 0).astype(jnp.bfloat16)


def attention_fwd(length, q, k, v):
    heads = q.shape[1] // HEAD_DIM
    return pl.pallas_call(
        fwd_kernel,
        in_specs=[SMEM, VMEM, VMEM, VMEM],
        out_specs=[VMEM, VMEM],
        out_shape=[
            jax.ShapeDtypeStruct(q.shape, jnp.bfloat16),
            jax.ShapeDtypeStruct((heads, BLK, BLK), jnp.bfloat16),
        ],
        compiler_params=params(FWD),
        cost_estimate=pl.CostEstimate(
            flops=heads * 4 * BLK * BLK * HEAD_DIM, bytes_accessed=6 << 20, transcendentals=heads * BLK * BLK
        ),
        name="attention_fwd",
    )(length, q, k, v)


def bwd_kernel(p_ref, q_ref, k_ref, v_ref, g_ref, dq_ref, dk_ref, dv_ref):
    for head in range(p_ref.shape[0]):
        cols = slice(head * HEAD_DIM, (head + 1) * HEAD_DIM)
        grad_keys, grad_values = [], []
        for first, keys in ((0, HALF), (HALF, BLK)):
            rows = slice(first, first + HALF)
            probs, grad = p_ref[head, rows, :keys], g_ref[rows, cols]
            grad_values.append(dot(probs, grad, 0, 0))
            grad_probs = dot(grad, v_ref[:keys, cols], 1, 1)
            wide = probs.astype(jnp.float32)
            centre = jnp.sum(wide * grad_probs, axis=-1, keepdims=True)
            grad_scores = (wide * (grad_probs - centre) * (1.0 / math.sqrt(HEAD_DIM))).astype(jnp.bfloat16)
            dq_ref[rows, cols] = dot(grad_scores, k_ref[:keys, cols], 1, 0).astype(jnp.bfloat16)
            grad_keys.append(dot(grad_scores, q_ref[rows, cols], 0, 0))
        for ref, (early, late) in ((dk_ref, grad_keys), (dv_ref, grad_values)):
            ref[:HALF, cols] = (early + late[:HALF]).astype(jnp.bfloat16)
            ref[HALF:, cols] = late[HALF:].astype(jnp.bfloat16)


def attention_bwd(probs, q, k, v, grad):
    heads = q.shape[1] // HEAD_DIM
    return pl.pallas_call(
        bwd_kernel,
        in_specs=[VMEM] * 5,
        out_specs=[VMEM] * 3,
        out_shape=[jax.ShapeDtypeStruct(q.shape, jnp.bfloat16)] * 3,
        compiler_params=params(BWD),
        cost_estimate=pl.CostEstimate(
            flops=heads * 8 * BLK * BLK * HEAD_DIM, bytes_accessed=6 << 20, transcendentals=0
        ),
        name="attention_bwd",
    )(probs, q, k, v, grad)


def unit_of(v, y_bit):
    return jnp.where(y_bit == 0, v, 7 - v)


def block_of(i, p):
    return 4 * jnp.where(i < 4, p[1], 1 - p[1]) + lax.rem(i, 4)


def place_here():
    return lax.axis_index("xh"), lax.axis_index("co"), lax.rem(lax.axis_index("y"), 2)


def own_copy(grad_ref, place, buf, sems):
    def copy(i):
        column = pl.multiple_of((2 * block_of(i, place) + place[0]) * BLK, BLK)
        return pltpu.make_async_copy(grad_ref.at[:, pl.ds(column, BLK)], buf.at[i], sems.at[i])

    return copy


def row_copy(ref, buf, sems, index=lambda i: i, out=False):
    def copy(i):
        rows = ref.at[pl.ds(pl.multiple_of(index(i) * BLK, BLK), BLK)]
        if out:
            return pltpu.make_async_copy(buf.at[i], rows, sems.at[i])
        return pltpu.make_async_copy(rows, buf.at[i], sems.at[i])

    return copy


def piece_copies(refs, buf, sems, place):
    def target(group, v):
        unit = unit_of(v, place[2])
        rows = pl.ds(pl.multiple_of(lax.rem(unit, 2) * HALF, HALF), HALF)
        return buf.at[4 * group + unit // 2, rows]

    def start(group):
        over_x, over_y = refs[2 * group], refs[2 * group + 1]

        def begin(v):
            pltpu.make_async_copy(over_x.at[v], target(group, v), sems.at[8 * group + v]).start()

        each(0, OVER_X, begin)
        for w in range(OVER_Y):
            pltpu.make_async_copy(over_y.at[w], target(group, 7 - w), sems.at[8 * group + 7 - w]).start()

    def wait(i):
        group = i // 4
        for half in range(2):
            v = unit_of(2 * lax.rem(i, 4) + half, place[2])
            there = target(group, v)
            pltpu.make_async_copy(there, there, sems.at[8 * group + v]).wait()

    return start, wait, target


def each(first, count, step):
    def body(i, carry):
        step(i)
        return carry

    lax.fori_loop(first, first + count, body, 0)


def pick_kernel(grad_ref, out_ref, sems):
    x_hi, core, y_bit = place_here()

    def copy(v):
        unit = unit_of(v, y_bit)
        rows = pl.ds(pl.multiple_of(lax.rem(unit, 2) * HALF, HALF), HALF)
        column = pl.multiple_of((2 * (4 * core + unit // 2) + 1 - x_hi) * BLK, BLK)
        return pltpu.make_async_copy(grad_ref.at[rows, pl.ds(column, BLK)], out_ref.at[v], sems.at[v])

    each(0, OVER_X, lambda v: copy(v).start())
    each(0, OVER_X, lambda v: copy(v).wait())


def pick_units(out_grad):
    return pl.pallas_call(
        pick_kernel,
        in_specs=[HBM],
        out_specs=VMEM,
        scratch_shapes=[pltpu.SemaphoreType.DMA((OVER_X,))],
        out_shape=jax.ShapeDtypeStruct((OVER_X, HALF, BLK), jnp.bfloat16),
        compiler_params=params(60),
        name="pick_units",
    )(out_grad)


def grad_kernel(grad_ref, near, far, last_ref, w_ref, scale_ref, out_ref, *scratch):
    own_buf, w_buf, piece_buf, acc_ref, own_sems, w_sems, piece_sems = scratch
    place = place_here()
    own = own_copy(grad_ref, place, own_buf, own_sems)
    weight = row_copy(w_ref, w_buf, w_sems, lambda i: block_of(i, place))
    last = [last_ref.at[pl.ds(group * OVER_Y, OVER_Y)] for group in range(2)]
    start, wait, _ = piece_copies((near, last[0], far, last[1]), piece_buf, piece_sems, place)
    own(0).start()
    weight(0).start()
    start(0)

    def begin(i):
        own(i).start()
        weight(i).start()

    each(1, 7, begin)
    start(1)
    acc_ref[...] = jnp.zeros_like(acc_ref)

    def step(i):
        own(i).wait()
        weight(i).wait()
        wait(i)
        w = w_buf[i]
        acc_ref[0] += dot(own_buf[i], w, 1, 1)
        acc_ref[1] += dot(piece_buf[i], w, 1, 1)

    each(0, 8, step)
    scale = scale_ref[...]
    x_hi = place[0]
    out_ref[x_hi] = (acc_ref[0] * scale).astype(jnp.bfloat16)
    out_ref[1 - x_hi] = (acc_ref[1] * scale).astype(jnp.bfloat16)


def grad_dot(out_grad, near, far, last, weights, scale):
    blocks = pltpu.VMEM((8, BLK, BLK), jnp.bfloat16)
    return pl.pallas_call(
        grad_kernel,
        in_specs=[HBM, ANY, ANY, ANY, HBM, VMEM],
        out_specs=VMEM,
        scratch_shapes=[
            blocks,
            blocks,
            blocks,
            pltpu.VMEM((2, BLK, BLK), jnp.float32),
            pltpu.SemaphoreType.DMA((8,)),
            pltpu.SemaphoreType.DMA((8,)),
            pltpu.SemaphoreType.DMA((16,)),
        ],
        out_shape=jax.ShapeDtypeStruct((2, BLK, BLK), jnp.bfloat16),
        compiler_params=params(54),
        cost_estimate=pl.CostEstimate(
            flops=4 * BLK * BLK * BLK * 8, bytes_accessed=13 << 20, transcendentals=0
        ),
        name="grad_dot",
    )(out_grad, near, far, last, weights, scale)


def own_kernel(a_ref, grad_ref, out_ref, at_ref, in_buf, out_buf, in_sems, out_sems):
    place = place_here()
    own = own_copy(grad_ref, place, in_buf, in_sems)
    out = row_copy(out_ref, out_buf, out_sems, out=True)
    each(0, 8, lambda i: own(i).start())
    at_ref[...] = a_ref[...].T

    def step(i):
        own(i).wait()
        out_buf[i] = dot(at_ref[...], in_buf[i], 1, 0).astype(jnp.bfloat16)
        out(i).start()

    each(0, 8, step)
    each(0, 8, lambda i: out(i).wait())


def own_dot(rotated, out_grad):
    blocks = pltpu.VMEM((8, BLK, BLK), jnp.bfloat16)
    return pl.pallas_call(
        own_kernel,
        in_specs=[VMEM, HBM],
        out_specs=ANY,
        scratch_shapes=[
            pltpu.VMEM((BLK, BLK), jnp.bfloat16),
            blocks,
            blocks,
            pltpu.SemaphoreType.DMA((8,)),
            pltpu.SemaphoreType.DMA((8,)),
        ],
        out_shape=jax.ShapeDtypeStruct((8 * BLK, BLK), jnp.bfloat16),
        compiler_params=params(24),
        cost_estimate=pl.CostEstimate(
            flops=2 * BLK * BLK * BLK * 8, bytes_accessed=9 << 20, transcendentals=0
        ),
        name="own_dot",
    )(rotated, out_grad)


def other_kernel(a_ref, own_ref, near, last, far, far_last, out_ref, keep_ref, *scratch):
    at_ref, own_buf, piece_buf, out_buf, own_sems, piece_sems, out_sems, a_sem, keep_sems = scratch
    place = place_here()
    load = pltpu.make_async_copy(a_ref, at_ref, a_sem)
    load.start()
    own = row_copy(own_ref, own_buf, own_sems)
    start, wait, target = piece_copies((near, last, far, far_last), piece_buf, piece_sems, place)
    out = row_copy(out_ref, out_buf, out_sems, lambda i: block_of(i, place), out=True)
    start(0)
    each(0, 8, lambda i: own(i).start())
    start(1)
    load.wait()
    at_ref[...] = at_ref[...].T

    def step(i):
        own(i).wait()
        wait(i)
        total = own_buf[i].astype(jnp.float32) + dot(at_ref[...], piece_buf[i], 1, 0)
        out_buf[i] = total.astype(jnp.bfloat16)
        out(i).start()

    keeps = []
    for group in range(2):
        each(4 * group, 4, step)
        for w in range(OVER_Y):
            at = group * OVER_Y + w
            keeps.append(pltpu.make_async_copy(target(group, 7 - w), keep_ref.at[at], keep_sems.at[at]))
            keeps[-1].start()
    each(0, 8, lambda i: out(i).wait())
    for keep in keeps:
        keep.wait()


def other_dot(rotated, own, near, last, far, far_last):
    blocks = pltpu.VMEM((8, BLK, BLK), jnp.bfloat16)
    return pl.pallas_call(
        other_kernel,
        in_specs=[ANY, ANY, *[ANY] * 4],
        out_specs=[HBM, HBM],
        scratch_shapes=[
            pltpu.VMEM((BLK, BLK), jnp.bfloat16),
            blocks,
            blocks,
            blocks,
            pltpu.SemaphoreType.DMA((8,)),
            pltpu.SemaphoreType.DMA((16,)),
            pltpu.SemaphoreType.DMA((8,)),
            pltpu.SemaphoreType.DMA,
            pltpu.SemaphoreType.DMA((2 * OVER_Y,)),
        ],
        out_shape=[
            pltpu.HBM((8 * BLK, BLK), jnp.bfloat16),
            pltpu.HBM((2 * OVER_Y, HALF, BLK), jnp.bfloat16),
        ],
        compiler_params=params(24),
        cost_estimate=pl.CostEstimate(
            flops=2 * BLK * BLK * BLK * 8, bytes_accessed=13 << 20, transcendentals=0
        ),
        name="other_dot",
    )(rotated, own, near, last, far, far_last)


def mix_kernel(parts, copies, x_ref, out_ref):
    x = x_ref[...].astype(jnp.float32)
    rows = x.shape[0] // parts
    total = x[:rows]
    for part in range(1, parts):
        total = total + x[part * rows : (part + 1) * rows]
    tokens = rows // 16
    blocks = [
        [total[s * tokens : (s + 1) * tokens, c * HEAD_DIM : (c + 1) * HEAD_DIM] for c in range(4)]
        for s in range(16)
    ]
    flat = [blocks[s][c] for s in range(16) for c in range(4)]
    step = 1
    while step < 64:
        flat = [
            flat[i] + flat[i + step] if not i & step else flat[i - step] - flat[i]
            for i in range(64)
        ]
        step *= 2
    for s in range(16):
        for c in range(4):
            mixed = (flat[s * 4 + c] * (1.0 / math.sqrt(HEADS))).astype(jnp.bfloat16)
            for copy in range(copies):
                first = copy * rows + s * tokens
                out_ref[first : first + tokens, c * HEAD_DIM : (c + 1) * HEAD_DIM] = mixed


def mix(x, parts, copies):
    return pl.pallas_call(
        functools.partial(mix_kernel, parts, copies),
        out_shape=jax.ShapeDtypeStruct((x.shape[0] // parts * copies, x.shape[1]), jnp.bfloat16),
        compiler_params=params(16),
        name="mix",
    )(x)


def body(queries, keys, values, out_grad, o_weight, exponents, valid_lengths):
    scale = jnp.exp2(exponents.astype(jnp.float32))

    weights = lax.all_gather(o_weight, "z", axis=0, tiled=True)

    across = [(h * 2 + l, (1 - h) * 2 + 1 - l) for h in range(2) for l in range(2)]
    swap, pairs = [(0, 1), (1, 0)], [(0, 1), (1, 0), (2, 3), (3, 2)]

    picked = pick_units(out_grad)
    near = lax.ppermute(picked, ("xh", "xl"), across)

    queries, _ = lax.optimization_barrier((queries, picked))
    attended, probs = attention_fwd(valid_lengths, queries, keys, values)
    turned = lax.all_to_all(attended, TENSOR, 0, 0, tiled=True)
    rotated = lax.all_to_all(mix(turned, 1, 1), TENSOR, 0, 0, tiled=True)
    rotated_other = lax.ppermute(rotated, "xh", swap)
    near, rotated = lax.optimization_barrier((near, rotated))
    last = lax.ppermute(near[:OVER_Y], "y", pairs)
    far = lax.ppermute(near, "co", swap)
    own = own_dot(rotated, out_grad)
    last, far, own = lax.optimization_barrier((last, far, own))
    far_last = lax.ppermute(last, "co", swap)
    partial, kept = other_dot(rotated_other, own, near, last, far, far_last)
    summed = lax.psum_scatter(partial, "z", scatter_dimension=0, tiled=True)

    grad_rotated = grad_dot(out_grad, near, far, kept, weights, scale[None, :])
    turned = lax.all_to_all(grad_rotated.reshape(2 * BLK, BLK), ("xh",) + TENSOR, 0, 0, tiled=True)
    grad_attended = lax.all_to_all(mix(turned, 2, 1), TENSOR, 0, 0, tiled=True)
    grad_query, grad_key, grad_value = attention_bwd(probs, queries, keys, values, grad_attended)

    grad_weight = summed.astype(jnp.float32) * scale[:, None]
    return grad_query, grad_key, grad_value, grad_weight


def solution(mesh):
    fine = Mesh(mesh.devices.reshape(8, 2, 4, 2, 2), DP + TENSOR)
    return jax.shard_map(
        body,
        mesh=fine,
        in_specs=(
            P(DP, TENSOR),
            P(DP, TENSOR),
            P(DP, TENSOR),
            P(DP, None),
            P(TENSOR, DP),
            P(TENSOR),
            P(DP),
        ),
        out_specs=(P(DP, TENSOR), P(DP, TENSOR), P(DP, TENSOR), P(TENSOR, DP)),
        check_vma=False,
    )
```

time: 144 us -> 140 us (0.972)
  Pallas kernels: 37.4 us -> 31.5 us
  starting transfers between devices: 6.5 us -> 9.41 us
    pallas_call x5 -> x6, Pallas kernels: 36.4 us -> 30.5 us  [the longest x1 9.43 us: grad_dot(): pl.pallas_call(grad_kernel, in_specs=[HBM, ANY, ANY, ANY, HBM, VMEM], out...]
    ppermute x1, waiting for transfers between devices: 5.44 us -> 2.31 us  [body(): last = lax.ppermute(near[:OVER_Y], 'y', pairs)]
    reduce_scatter x1, waiting for transfers between devices: 2.42 us -> 5.14 us  [body(): summed = lax.psum_scatter(partial, 'z', scatter_dimension=0, tiled=True)]
    unnamed x12 -> x26, local copies, waits for them, and re-layouts: 2.6 us -> 4.18 us
    ppermute x1, starting transfers between devices: 0.01 us -> 1.58 us  [body(): last = lax.ppermute(near[:OVER_Y], 'y', pairs)]
    another operation x1 -> x0, local copies, waits for them, and re-layouts: 1.48 us -> none  [body(): jnp.stack([lax.dynamic_slice(out_grad, (0, (2 * (4 * core + y_bit + i) +...]
  transfers between devices with their start and end apart: 7 -> 7, of which waited for: 4 -> 4; matrix products, arithmetic and copies ran while one was open for 3% -> 0% of each run, Pallas kernels for 26% -> 23%
where the time goes in v3:
time: 140 us; the launch traced here: 139 us
  blocking collectives  66.3 us (47%)
  Pallas kernels  31.5 us (22%)
  between operations  14.9 us (11%)
  waiting for transfers between devices  10.2 us (7%)
  starting transfers between devices  9.41 us (7%)
  local copies, waits for them, and re-layouts  4.21 us (3%)
  other arithmetic  2.73 us (2%)
    all_to_all x1, blocking collectives, body(): lax.all_to_all(grad_rotated.reshape(2 * BLK, BLK), ('xh',) + TENSOR, 0, 0...  24.7 us
    all_to_all x1, blocking collectives, body(): turned = lax.all_to_all(attended, TENSOR, 0, 0, tiled=True)  15.1 us
    all_to_all x1, blocking collectives, body(): rotated = lax.all_to_all(mix(turned, 1, 1), TENSOR, 0, 0, tiled=True)  13.5 us
    all_to_all x1, blocking collectives, body(): grad_attended = lax.all_to_all(mix(turned, 2, 1), TENSOR, 0, 0, tiled=True)  13 us
    pallas_call x1, Pallas kernels, grad_dot(): pl.pallas_call(grad_kernel, in_specs=[HBM, ANY, ANY, ANY, HBM, VMEM], out...  9.43 us
    pallas_call x1, Pallas kernels, other_dot(): pl.pallas_call(other_kernel, in_specs=[ANY, ANY, *[ANY] * 4], out_specs=[...  5.8 us
    reduce_scatter x1, waiting for transfers between devices, body(): summed = lax.psum_scatter(partial, 'z', scatter_dimension=0, tiled=True)  5.14 us
    pallas_call x1, Pallas kernels, own_dot(): pl.pallas_call(own_kernel, in_specs=[VMEM, HBM], out_specs=ANY, scratch_s...  4.91 us
  transfers between devices with their start and end apart: 7, of which 4 were waited for; matrix products, arithmetic and copies ran while one was open for 0% of the time, Pallas kernels for 23%

profile of v3, /device:TPU:1, one launch (start us, length us, event | category | flops | bytes accessed | tf_op | source)
XLA Modules:
  0.0 139.2 jit_solution(13634853719329226075)
XLA Ops:
  7.2 0.7 all-gather.2.cloned.1.call-update
  8.0 2.7 %pick_units.1 = bf16[6,256,512]{2,1,0:T(8,128)(2,1)} custom-call(bf16[512,8192]{1,0:T(8,128)(2,1)} %grad_ref.5), custom_call_target="tpu_custom_call" | custom-call | tf_op jit(solution)/shard_map/pick_units/pallas_call | solution.py:185
  10.7 3.4 %collective-permute-start = (bf16[6,256,512]{2,1,0:T(8,128)(2,1)}, bf16[6,256,512]{2,1,0:T(8,128)(2,1)S(1)}, u32[]{:S(2)}, u32[]{:S(2)}) collective-permute-start(bf16[6,256,512]{2,1,0:T(8,128)(2,1)} %pick_units.1), channel_id=1, source_target_pairs={{0,18},{2,16},{16,2},{18,0},{1,19},{3,17},{17,3},{19,1},{4,22},{6,... | collective-permute-start | bytes 4718600 | tf_op jit(solution)/shard_map/ppermute | solution.py:399
  14.8 3.5 %attention_fwd.1 = (bf16[512,512]{1,0:T(8,128)(2,1)S(1)}, bf16[4,512,512]{2,1,0:T(8,128)(2,1)S(1)}) custom-call(s32[1]{0:T(128)S(6)} %copy.11.len_ref, bf16[512,512]{1,0:T(8,128)(2,1)S(1)} %copy-done.5, bf16[512,512]{1,0:T(8,128)(2,1)S(1)} %copy-done.7, bf16[512,512]{1,0:T(8,128)(2,1)S(1)} %copy-done.9), custom_call_target="tpu_custom_call" | custom-call | flops 536870912 | bytes 6291456 | tf_op jit(solution)/shard_map/attention_fwd/pallas_call | solution.py:57
  18.3 15.1 %all_to_all.45 = bf16[16,32,512]{2,1,0:T(8,128)(2,1)S(1)} all-to-all(bf16[16,32,512]{2,1,0:T(8,128)(2,1)S(1)} %bitcast.16), channel_id=1, replica_groups=mesh['z'=8,'xh'=2,'y'=4,'xl'=2,'co'=2] {'y','xl','co'}, dimensions={0} | all-to-all | bytes 1048576 | tf_op jit(solution)/shard_map/all_to_all | solution.py:403
  33.8 13.5 %all_to_all.46 = bf16[16,32,512]{2,1,0:T(8,128)(2,1)S(1)} all-to-all(bf16[16,32,512]{2,1,0:T(8,128)(2,1)S(1)} %bitcast.14), channel_id=1, replica_groups=mesh['z'=8,'xh'=2,'y'=4,'xl'=2,'co'=2] {'y','xl','co'}, dimensions={0} | all-to-all | bytes 1048576 | tf_op jit(solution)/shard_map/all_to_all | solution.py:404
  47.5 2.2 %collective-permute-start.2 = (bf16[6,256,512]{2,1,0:T(8,128)(2,1)S(1)}, bf16[6,256,512]{2,1,0:T(8,128)(2,1)S(1)}, u32[]{:S(2)}, u32[]{:S(2)}) collective-permute-start(bf16[6,256,512]{2,1,0:T(8,128)(2,1)S(1)} %collective-permute-done.near), channel_id=1, source_target_pairs={{0,1},{1,0},{2,3},{3,2},{4,5},{5,4},{6,7},{7,6},{8,9},{9,8},{10,11... | collective-permute-start | bytes 4718600 | tf_op jit(solution)/shard_map/ppermute | solution.py:408
  49.7 1.6 %collective-permute-start.1 = (bf16[2,256,512]{2,1,0:T(8,128)(2,1)S(1)}, bf16[2,256,512]{2,1,0:T(8,128)(2,1)S(1)}, u32[]{:S(2)}, u32[]{:S(2)}) collective-permute-start(bf16[2,256,512]{2,1,0:T(8,128)(2,1)S(1)} %slice.3), channel_id=1, source_target_pairs={{0,4},{4,0},{8,12},{12,8},{1,5},{5,1},{9,13},{13,9},{2,6},{6,2},{1... | collective-permute-start | bytes 1572872 | tf_op jit(solution)/shard_map/ppermute | solution.py:407
  51.3 1.5 %collective-permute-start.3 = (bf16[512,512]{1,0:T(8,128)(2,1)S(1)}, bf16[512,512]{1,0:T(8,128)(2,1)S(1)}, u32[]{:S(2)}, u32[]{:S(2)}) collective-permute-start(bf16[512,512]{1,0:T(8,128)(2,1)S(1)} %bitcast.10), channel_id=1, source_target_pairs={{0,16},{16,0},{1,17},{17,1},{2,18},{18,2},{3,19},{19,3},{4,20},{20... | collective-permute-start | bytes 1572872 | tf_op jit(solution)/shard_map/ppermute | solution.py:405
  52.8 3.5 %copy-done = bf16[512,8192]{1,0:T(8,128)(2,1)S(1)} copy-done((bf16[512,8192]{1,0:T(8,128)(2,1)S(1)}, bf16[512,8192]{1,0:T(8,128)(2,1)}, u32[]{:S(2)}) %copy-start) | copy-done | bytes 8388632
  56.3 4.9 %own_dot.1.own_ref = bf16[4096,512]{1,0:T(8,128)(2,1)S(1)} custom-call(bf16[512,512]{1,0:T(8,128)(2,1)S(1)} %bitcast.11, bf16[512,8192]{1,0:T(8,128)(2,1)S(1)} %copy-done), custom_call_target="tpu_custom_call" | custom-call | flops 2147483648 | bytes 9437184 | tf_op jit(solution)/shard_map/own_dot/pallas_call | solution.py:272
  61.2 2.3 %collective-permute-done.1.last = bf16[2,256,512]{2,1,0:T(8,128)(2,1)S(1)} collective-permute-done((bf16[2,256,512]{2,1,0:T(8,128)(2,1)S(1)}, bf16[2,256,512]{2,1,0:T(8,128)(2,1)S(1)}, u32[]{:S(2)}, u32[]{:S(2)}) %collective-permute-start.1) | collective-permute-done | bytes 524320 | tf_op jit(solution)/shard_map/ppermute | solution.py:407
  63.5 0.6 collective-permute-start.4
  64.2 1.9 %collective-permute-done.3.a_ref = bf16[512,512]{1,0:T(8,128)(2,1)S(1)} collective-permute-done((bf16[512,512]{1,0:T(8,128)(2,1)S(1)}, bf16[512,512]{1,0:T(8,128)(2,1)S(1)}, u32[]{:S(2)}, u32[]{:S(2)}) %collective-permute-start.3) | collective-permute-done | bytes 524320 | tf_op jit(solution)/shard_map/ppermute | solution.py:405
  66.0 5.8 %other_dot.1 = (bf16[4096,512]{1,0:T(8,128)(2,1)}, bf16[4,256,512]{2,1,0:T(8,128)(2,1)}) custom-call(bf16[512,512]{1,0:T(8,128)(2,1)S(1)} %collective-permute-done.3.a_ref, bf16[4096,512]{1,0:T(8,128)(2,1)S(1)} %own_dot.1.own_ref, bf16[6,256,512]{2,1,0:T(8,128)(2,1)S(1)} %collective-permute-done.near, bf16[2,256,512]{2,1,0:T(8,128)(2,1)S(1)} %collective-permute-done.1.last, ...), custom_call_target="tpu_custom_call" | custom-call | flops 2147483648 | bytes 13631488 | tf_op jit(solution)/shard_map/other_dot/pallas_call | solution.py:327
  71.9 0.6 copy-done.12
  72.5 0.6 multiply_exponential_fusion
  73.1 9.4 %grad_dot.1 = bf16[2,512,512]{2,1,0:T(8,128)(2,1)} custom-call(bf16[512,8192]{1,0:T(8,128)(2,1)} %grad_ref.5, bf16[6,256,512]{2,1,0:T(8,128)(2,1)} %copy-done.1, bf16[6,256,512]{2,1,0:T(8,128)(2,1)} %copy-done.2, bf16[4,256,512]{2,1,0:T(8,128)(2,1)} %get-tuple-element.25.last_ref, bf16[4096,512]{1,0:T(8,128)(2,1)} %all-gather.2.cloned.1.call-done.w_ref, ...), custom_call_target="tpu_custom_call" | custom-call | flops 4294967296 | bytes 13631488 | tf_op jit(solution)/shard_map/grad_dot/pallas_call | solution.py:232
  82.6 24.7 %all_to_all.47 = bf16[32,32,512]{2,1,0:T(8,128)(2,1)S(1)} all-to-all(bf16[32,32,512]{2,1,0:T(8,128)(2,1)} %bitcast.17), channel_id=1, replica_groups=mesh['z'=8,'xh'=2,'y'=4,'xl'=2,'co'=2] {'xh','y','xl','co'}, dimensions={0} | all-to-all | bytes 2097152 | tf_op jit(solution)/shard_map/all_to_all | solution.py:416
  107.3 0.5 mix.3
  107.8 13.0 %all_to_all.48 = bf16[16,32,512]{2,1,0:T(8,128)(2,1)S(1)} all-to-all(bf16[16,32,512]{2,1,0:T(8,128)(2,1)S(1)} %bitcast.12), channel_id=1, replica_groups=mesh['z'=8,'xh'=2,'y'=4,'xl'=2,'co'=2] {'y','xl','co'}, dimensions={0} | all-to-all | bytes 1048576 | tf_op jit(solution)/shard_map/all_to_all | solution.py:417
  120.9 4.2 %attention_bwd.1 = (bf16[512,512]{1,0:T(8,128)(2,1)}, bf16[512,512]{1,0:T(8,128)(2,1)}, bf16[512,512]{1,0:T(8,128)(2,1)}) custom-call(bf16[4,512,512]{2,1,0:T(8,128)(2,1)S(1)} %copy-done.4, bf16[512,512]{1,0:T(8,128)(2,1)S(1)} %copy-done.6, bf16[512,512]{1,0:T(8,128)(2,1)S(1)} %copy-done.8, bf16[512,512]{1,0:T(8,128)(2,1)S(1)} %copy-done.10, ...), custom_call_target="tpu_custom_call" | custom-call | flops 1073741824 | bytes 6291456 | tf_op jit(solution)/shard_map/attention_bwd/pallas_call | solution.py:94
  125.1 5.1 %reduce-scatter.2.cloned.1.call-done = bf16[512,512]{1,0:T(8,128)(2,1)} async-done(((bf16[4096,512]{1,0:T(8,128)(2,1)}), bf16[512,512]{1,0:T(8,128)(2,1)}) %reduce-scatter.2.cloned.1.call-update) | async-done | bytes 524304 | tf_op jit(solution)/shard_map/reduce_scatter | solution.py:413
  130.2 2.1 %convert_multiply_fusion = f32[512,512]{1,0:T(8,128)} fusion(bf16[512,512]{1,0:T(8,128)(2,1)} %reduce-scatter.2.cloned.1.call-done, f32[512]{0:T(512)S(1)} %copy-done.11), kind=kLoop, calls=%fused_computation | loop fusion | flops 524288 | bytes 1574912 | tf_op jit(solution)/shard_map/mul | solution.py:420
  (33 shorter events, 0.9 us)
Async XLA Ops:
  7.2 65.9 %all-gather.2.cloned.1.call-start = ((), (), s32[]{:S(2)}) async-start(), calls=%async_computation.5 | async-start | bytes 4718592 | tf_op jit(solution)/shard_map/all_gather | solution.py:393
  7.9 6.8 %copy-start.5 = (bf16[512,512]{1,0:T(8,128)(2,1)S(1)}, bf16[512,512]{1,0:T(8,128)(2,1)}, u32[]{:S(2)}) copy-start(bf16[512,512]{1,0:T(8,128)(2,1)} %q_ref.1) | copy-start | bytes 1572868
  7.9 6.8 %copy-start.7 = (bf16[512,512]{1,0:T(8,128)(2,1)S(1)}, bf16[512,512]{1,0:T(8,128)(2,1)}, u32[]{:S(2)}) copy-start(bf16[512,512]{1,0:T(8,128)(2,1)} %k_ref.3) | copy-start | bytes 1572868
  7.9 6.8 %copy-start.9 = (bf16[512,512]{1,0:T(8,128)(2,1)S(1)}, bf16[512,512]{1,0:T(8,128)(2,1)}, u32[]{:S(2)}) copy-start(bf16[512,512]{1,0:T(8,128)(2,1)} %v_ref.3) | copy-start | bytes 1572868
  7.9 122.3 %reduce-scatter.2.cloned.1.call-start = ((), (), s32[]{:S(2)}) async-start(), calls=%async_computation.6 | async-start | bytes 4718592 | tf_op jit(solution)/shard_map/reduce_scatter | solution.py:413
  10.7 36.8 %collective-permute-start = (bf16[6,256,512]{2,1,0:T(8,128)(2,1)}, bf16[6,256,512]{2,1,0:T(8,128)(2,1)S(1)}, u32[]{:S(2)}, u32[]{:S(2)}) collective-permute-start(bf16[6,256,512]{2,1,0:T(8,128)(2,1)} %pick_units.1), channel_id=1, source_target_pairs={{0,18},{2,16},{16,2},{18,0},{1,19},{3,17},{17,3},{19,1},{4,22},{6,... | collective-permute-start | bytes 4718600 | tf_op jit(solution)/shard_map/ppermute | solution.py:399
  18.2 33.0 %copy-start.3 = (bf16[4,512,512]{2,1,0:T(8,128)(2,1)}, bf16[4,512,512]{2,1,0:T(8,128)(2,1)S(1)}, u32[]{:S(2)}) copy-start(bf16[4,512,512]{2,1,0:T(8,128)(2,1)S(1)} %get-tuple-element.18.p_ref) | copy-start | bytes 6291460
  47.5 18.5 %copy-start.1 = (bf16[6,256,512]{2,1,0:T(8,128)(2,1)}, bf16[6,256,512]{2,1,0:T(8,128)(2,1)S(1)}, u32[]{:S(2)}) copy-start(bf16[6,256,512]{2,1,0:T(8,128)(2,1)S(1)} %collective-permute-done.near) | copy-start | bytes 4718596
  47.5 16.0 %collective-permute-start.2 = (bf16[6,256,512]{2,1,0:T(8,128)(2,1)S(1)}, bf16[6,256,512]{2,1,0:T(8,128)(2,1)S(1)}, u32[]{:S(2)}, u32[]{:S(2)}) collective-permute-start(bf16[6,256,512]{2,1,0:T(8,128)(2,1)S(1)} %collective-permute-done.near), channel_id=1, source_target_pairs={{0,1},{1,0},{2,3},{3,2},{4,5},{5,4},{6,7},{7,6},{8,9},{9,8},{10,11... | collective-permute-start | bytes 4718600 | tf_op jit(solution)/shard_map/ppermute | solution.py:408
  49.7 13.8 %collective-permute-start.1 = (bf16[2,256,512]{2,1,0:T(8,128)(2,1)S(1)}, bf16[2,256,512]{2,1,0:T(8,128)(2,1)S(1)}, u32[]{:S(2)}, u32[]{:S(2)}) collective-permute-start(bf16[2,256,512]{2,1,0:T(8,128)(2,1)S(1)} %slice.3), channel_id=1, source_target_pairs={{0,4},{4,0},{8,12},{12,8},{1,5},{5,1},{9,13},{13,9},{2,6},{6,2},{1... | collective-permute-start | bytes 1572872 | tf_op jit(solution)/shard_map/ppermute | solution.py:407
  51.3 14.7 %collective-permute-start.3 = (bf16[512,512]{1,0:T(8,128)(2,1)S(1)}, bf16[512,512]{1,0:T(8,128)(2,1)S(1)}, u32[]{:S(2)}, u32[]{:S(2)}) collective-permute-start(bf16[512,512]{1,0:T(8,128)(2,1)S(1)} %bitcast.10), channel_id=1, source_target_pairs={{0,16},{16,0},{1,17},{17,1},{2,18},{18,2},{3,19},{19,3},{4,20},{20... | collective-permute-start | bytes 1572872 | tf_op jit(solution)/shard_map/ppermute | solution.py:405
  52.8 3.5 %copy-start = (bf16[512,8192]{1,0:T(8,128)(2,1)S(1)}, bf16[512,8192]{1,0:T(8,128)(2,1)}, u32[]{:S(2)}) copy-start(bf16[512,8192]{1,0:T(8,128)(2,1)} %grad_ref.5) | copy-start | bytes 25165828
  63.5 8.3 %copy-start.2 = (bf16[6,256,512]{2,1,0:T(8,128)(2,1)}, bf16[6,256,512]{2,1,0:T(8,128)(2,1)S(1)}, u32[]{:S(2)}) copy-start(bf16[6,256,512]{2,1,0:T(8,128)(2,1)S(1)} %collective-permute-done.2.far) | copy-start | bytes 4718596
  63.5 2.5 %collective-permute-start.4 = (bf16[2,256,512]{2,1,0:T(8,128)(2,1)S(1)}, bf16[2,256,512]{2,1,0:T(8,128)(2,1)S(1)}, u32[]{:S(2)}, u32[]{:S(2)}) collective-permute-start(bf16[2,256,512]{2,1,0:T(8,128)(2,1)S(1)} %collective-permute-done.1.last), channel_id=1, source_target_pairs={{0,1},{1,0},{2,3},{3,2},{4,5},{5,4},{6,7},{7,6},{8,9},{9,8},{10,11... | collective-permute-start | bytes 1572872 | tf_op jit(solution)/shard_map/ppermute | solution.py:411
  71.8 0.7 copy-start.12
  82.5 38.3 %copy-start.4 = (bf16[4,512,512]{2,1,0:T(8,128)(2,1)S(1)}, bf16[4,512,512]{2,1,0:T(8,128)(2,1)}, u32[]{:S(2)}) copy-start(bf16[4,512,512]{2,1,0:T(8,128)(2,1)} %copy-done.3) | copy-start | bytes 6291460
  82.6 38.3 %copy-start.6 = (bf16[512,512]{1,0:T(8,128)(2,1)S(1)}, bf16[512,512]{1,0:T(8,128)(2,1)}, u32[]{:S(2)}) copy-start(bf16[512,512]{1,0:T(8,128)(2,1)} %q_ref.1) | copy-start | bytes 1572868
  82.6 38.3 %copy-start.8 = (bf16[512,512]{1,0:T(8,128)(2,1)S(1)}, bf16[512,512]{1,0:T(8,128)(2,1)}, u32[]{:S(2)}) copy-start(bf16[512,512]{1,0:T(8,128)(2,1)} %k_ref.3) | copy-start | bytes 1572868
  82.6 38.3 %copy-start.10 = (bf16[512,512]{1,0:T(8,128)(2,1)S(1)}, bf16[512,512]{1,0:T(8,128)(2,1)}, u32[]{:S(2)}) copy-start(bf16[512,512]{1,0:T(8,128)(2,1)} %v_ref.3) | copy-start | bytes 1572868
  82.6 47.7 %copy-start.11 = (f32[512]{0:T(512)S(1)}, f32[512]{0:T(512)}, u32[]{:S(2)}) copy-start(f32[512]{0:T(512)} %multiply_exponential_fusion) | copy-start | bytes 6148
Sparse Core Ops, SparseCore 0:
  9.8 58.6 all-gather.1
  72.0 58.2 reduce-scatter.1

commit v4 on v3

--- a/solution.py
+++ b/solution.py
@@ -20,8 +20,9 @@
 HBM = pl.BlockSpec(memory_space=pltpu.HBM)
 SMEM = pl.BlockSpec(memory_space=pltpu.SMEM)
 VMEM = pl.BlockSpec(memory_space=pltpu.VMEM)
-FWD, BWD = 24, 24
+FWD, BWD = 18, 18
 OVER_X = 6
+BLOCKS = jax.ShapeDtypeStruct((8, BLK, BLK), jnp.bfloat16)
 OVER_Y = 8 - OVER_X
 
 
@@ -116,24 +117,6 @@
     return lax.axis_index("xh"), lax.axis_index("co"), lax.rem(lax.axis_index("y"), 2)
 
 
-def own_copy(grad_ref, place, buf, sems):
-    def copy(i):
-        column = pl.multiple_of((2 * block_of(i, place) + place[0]) * BLK, BLK)
-        return pltpu.make_async_copy(grad_ref.at[:, pl.ds(column, BLK)], buf.at[i], sems.at[i])
-
-    return copy
-
-
-def row_copy(ref, buf, sems, index=lambda i: i, out=False):
-    def copy(i):
-        rows = ref.at[pl.ds(pl.multiple_of(index(i) * BLK, BLK), BLK)]
-        if out:
-            return pltpu.make_async_copy(buf.at[i], rows, sems.at[i])
-        return pltpu.make_async_copy(rows, buf.at[i], sems.at[i])
-
-    return copy
-
-
 def piece_copies(refs, buf, sems, place):
     def target(group, v):
         unit = unit_of(v, place[2])
@@ -193,162 +176,130 @@
     )(out_grad)
 
 
-def grad_kernel(grad_ref, near, far, last_ref, w_ref, scale_ref, out_ref, *scratch):
-    own_buf, w_buf, piece_buf, acc_ref, own_sems, w_sems, piece_sems = scratch
-    place = place_here()
-    own = own_copy(grad_ref, place, own_buf, own_sems)
-    weight = row_copy(w_ref, w_buf, w_sems, lambda i: block_of(i, place))
-    last = [last_ref.at[pl.ds(group * OVER_Y, OVER_Y)] for group in range(2)]
-    start, wait, _ = piece_copies((near, last[0], far, last[1]), piece_buf, piece_sems, place)
-    own(0).start()
-    weight(0).start()
-    start(0)
-
-    def begin(i):
-        own(i).start()
-        weight(i).start()
-
-    each(1, 7, begin)
-    start(1)
-    acc_ref[...] = jnp.zeros_like(acc_ref)
-
-    def step(i):
-        own(i).wait()
-        weight(i).wait()
-        wait(i)
-        w = w_buf[i]
-        acc_ref[0] += dot(own_buf[i], w, 1, 1)
-        acc_ref[1] += dot(piece_buf[i], w, 1, 1)
-
-    each(0, 8, step)
+def take_kernel(grad_ref, out_ref, sems):
+    x_hi, _, _ = place_here()
+
+    def copy(z):
+        column = pl.multiple_of((2 * z + x_hi) * BLK, BLK)
+        return pltpu.make_async_copy(grad_ref.at[:, pl.ds(column, BLK)], out_ref.at[z], sems.at[z])
+
+    each(0, 8, lambda z: copy(z).start())
+    each(0, 8, lambda z: copy(z).wait())
+
+
+def take_own(out_grad):
+    return pl.pallas_call(
+        take_kernel,
+        in_specs=[HBM],
+        out_specs=VMEM,
+        scratch_shapes=[pltpu.SemaphoreType.DMA((8,))],
+        out_shape=BLOCKS,
+        compiler_params=params(18),
+        cost_estimate=pl.CostEstimate(flops=0, bytes_accessed=8 << 20, transcendentals=0),
+        name="take_own",
+    )(out_grad)
+
+
+def z_at(offset):
+    return lax.rem(lax.axis_index("z") + offset, 8)
+
+
+def at_z(z, core):
+    return 4 * jnp.where(z // 4 == core, 0, 1) + lax.rem(z, 4)
+
+
+def grad_kernel(own_ref, pieces_ref, scale_ref, *refs):
+    w_refs, (out_ref, acc_ref) = refs[:9], refs[9:]
+    x_hi, core, _ = place_here()
     scale = scale_ref[...]
-    x_hi = place[0]
-    out_ref[x_hi] = (acc_ref[0] * scale).astype(jnp.bfloat16)
-    out_ref[1 - x_hi] = (acc_ref[1] * scale).astype(jnp.bfloat16)
-
-
-def grad_dot(out_grad, near, far, last, weights, scale):
-    blocks = pltpu.VMEM((8, BLK, BLK), jnp.bfloat16)
+    for r, offset in enumerate((0, 7, 1, 6, 2, 5, 3, 4)):
+        z = z_at(offset)
+        w = w_refs[r][...] if r < 7 else jnp.concatenate([w_refs[7][...], w_refs[8][...]])
+        mine = dot(own_ref[z], w, 1, 1)
+        theirs = dot(pieces_ref[at_z(z, core)], w, 1, 1)
+        if r == 0:
+            acc_ref[0], acc_ref[1] = mine, theirs
+        elif r < 7:
+            acc_ref[0] += mine
+            acc_ref[1] += theirs
+        else:
+            out_ref[x_hi] = ((acc_ref[0] + mine) * scale).astype(jnp.bfloat16)
+            out_ref[1 - x_hi] = ((acc_ref[1] + theirs) * scale).astype(jnp.bfloat16)
+
+
+def grad_dot(own_blocks, pieces, weights, scale):
     return pl.pallas_call(
         grad_kernel,
-        in_specs=[HBM, ANY, ANY, ANY, HBM, VMEM],
+        in_specs=[VMEM] * 12,
         out_specs=VMEM,
-        scratch_shapes=[
-            blocks,
-            blocks,
-            blocks,
-            pltpu.VMEM((2, BLK, BLK), jnp.float32),
-            pltpu.SemaphoreType.DMA((8,)),
-            pltpu.SemaphoreType.DMA((8,)),
-            pltpu.SemaphoreType.DMA((16,)),
-        ],
+        scratch_shapes=[pltpu.VMEM((2, BLK, BLK), jnp.float32)],
         out_shape=jax.ShapeDtypeStruct((2, BLK, BLK), jnp.bfloat16),
-        compiler_params=params(54),
+        compiler_params=params(18),
         cost_estimate=pl.CostEstimate(
             flops=4 * BLK * BLK * BLK * 8, bytes_accessed=13 << 20, transcendentals=0
         ),
         name="grad_dot",
-    )(out_grad, near, far, last, weights, scale)
-
-
-def own_kernel(a_ref, grad_ref, out_ref, at_ref, in_buf, out_buf, in_sems, out_sems):
-    place = place_here()
-    own = own_copy(grad_ref, place, in_buf, in_sems)
-    out = row_copy(out_ref, out_buf, out_sems, out=True)
-    each(0, 8, lambda i: own(i).start())
+    )(own_blocks, pieces, scale, *weights)
+
+
+def own_kernel(a_ref, own_ref, out_ref, at_ref):
     at_ref[...] = a_ref[...].T
 
-    def step(i):
-        own(i).wait()
-        out_buf[i] = dot(at_ref[...], in_buf[i], 1, 0).astype(jnp.bfloat16)
-        out(i).start()
+    def step(offset):
+        out_ref[offset] = dot(at_ref[...], own_ref[z_at(offset)], 1, 0).astype(jnp.bfloat16)
 
     each(0, 8, step)
-    each(0, 8, lambda i: out(i).wait())
-
-
-def own_dot(rotated, out_grad):
-    blocks = pltpu.VMEM((8, BLK, BLK), jnp.bfloat16)
+
+
+def own_dot(rotated, own_blocks):
     return pl.pallas_call(
         own_kernel,
-        in_specs=[VMEM, HBM],
-        out_specs=ANY,
-        scratch_shapes=[
-            pltpu.VMEM((BLK, BLK), jnp.bfloat16),
-            blocks,
-            blocks,
-            pltpu.SemaphoreType.DMA((8,)),
-            pltpu.SemaphoreType.DMA((8,)),
-        ],
-        out_shape=jax.ShapeDtypeStruct((8 * BLK, BLK), jnp.bfloat16),
-        compiler_params=params(24),
+        in_specs=[VMEM, VMEM],
+        out_specs=VMEM,
+        scratch_shapes=[pltpu.VMEM((BLK, BLK), jnp.bfloat16)],
+        out_shape=BLOCKS,
+        compiler_params=params(18),
         cost_estimate=pl.CostEstimate(
             flops=2 * BLK * BLK * BLK * 8, bytes_accessed=9 << 20, transcendentals=0
         ),
         name="own_dot",
-    )(rotated, out_grad)
-
-
-def other_kernel(a_ref, own_ref, near, last, far, far_last, out_ref, keep_ref, *scratch):
-    at_ref, own_buf, piece_buf, out_buf, own_sems, piece_sems, out_sems, a_sem, keep_sems = scratch
+    )(rotated, own_blocks)
+
+
+def other_kernel(a_ref, own_ref, near, last, far, far_last, *refs):
+    out_refs, (pieces_ref, at_ref, sems) = refs[:9], refs[9:]
     place = place_here()
-    load = pltpu.make_async_copy(a_ref, at_ref, a_sem)
-    load.start()
-    own = row_copy(own_ref, own_buf, own_sems)
-    start, wait, target = piece_copies((near, last, far, far_last), piece_buf, piece_sems, place)
-    out = row_copy(out_ref, out_buf, out_sems, lambda i: block_of(i, place), out=True)
+    start, wait, _ = piece_copies((near, last, far, far_last), pieces_ref, sems, place)
     start(0)
-    each(0, 8, lambda i: own(i).start())
     start(1)
-    load.wait()
-    at_ref[...] = at_ref[...].T
-
-    def step(i):
-        own(i).wait()
-        wait(i)
-        total = own_buf[i].astype(jnp.float32) + dot(at_ref[...], piece_buf[i], 1, 0)
-        out_buf[i] = total.astype(jnp.bfloat16)
-        out(i).start()
-
-    keeps = []
-    for group in range(2):
-        each(4 * group, 4, step)
-        for w in range(OVER_Y):
-            at = group * OVER_Y + w
-            keeps.append(pltpu.make_async_copy(target(group, 7 - w), keep_ref.at[at], keep_sems.at[at]))
-            keeps[-1].start()
-    each(0, 8, lambda i: out(i).wait())
-    for keep in keeps:
-        keep.wait()
+    at_ref[...] = a_ref[...].T
+    each(0, 8, wait)
+    for offset in (4, 3, 5, 2, 6, 1, 7, 0):
+        block = pieces_ref[at_z(z_at(offset), place[1])]
+        total = own_ref[offset].astype(jnp.float32) + dot(at_ref[...], block, 1, 0)
+        total = total.astype(jnp.bfloat16)
+        if offset == 4:
+            out_refs[4][...], out_refs[8][...] = total[:HALF], total[HALF:]
+        else:
+            out_refs[offset][...] = total
 
 
 def other_dot(rotated, own, near, last, far, far_last):
-    blocks = pltpu.VMEM((8, BLK, BLK), jnp.bfloat16)
-    return pl.pallas_call(
+    block = jax.ShapeDtypeStruct((BLK, BLK), jnp.bfloat16)
+    half = jax.ShapeDtypeStruct((HALF, BLK), jnp.bfloat16)
+    *terms, pieces = pl.pallas_call(
         other_kernel,
-        in_specs=[ANY, ANY, *[ANY] * 4],
-        out_specs=[HBM, HBM],
-        scratch_shapes=[
-            pltpu.VMEM((BLK, BLK), jnp.bfloat16),
-            blocks,
-            blocks,
-            blocks,
-            pltpu.SemaphoreType.DMA((8,)),
-            pltpu.SemaphoreType.DMA((16,)),
-            pltpu.SemaphoreType.DMA((8,)),
-            pltpu.SemaphoreType.DMA,
-            pltpu.SemaphoreType.DMA((2 * OVER_Y,)),
-        ],
-        out_shape=[
-            pltpu.HBM((8 * BLK, BLK), jnp.bfloat16),
-            pltpu.HBM((2 * OVER_Y, HALF, BLK), jnp.bfloat16),
-        ],
-        compiler_params=params(24),
+        in_specs=[VMEM, VMEM, *[ANY] * 4],
+        out_specs=[VMEM] * 10,
+        scratch_shapes=[pltpu.VMEM((BLK, BLK), jnp.bfloat16), pltpu.SemaphoreType.DMA((16,))],
+        out_shape=[half if offset in (4, 8) else block for offset in range(9)] + [BLOCKS],
+        compiler_params=params(18),
         cost_estimate=pl.CostEstimate(
             flops=2 * BLK * BLK * BLK * 8, bytes_accessed=13 << 20, transcendentals=0
         ),
         name="other_dot",
     )(rotated, own, near, last, far, far_last)
+    return terms, pieces
 
 
 def mix_kernel(parts, copies, x_ref, out_ref):
@@ -390,7 +341,12 @@
 def body(queries, keys, values, out_grad, o_weight, exponents, valid_lengths):
     scale = jnp.exp2(exponents.astype(jnp.float32))
 
-    weights = lax.all_gather(o_weight, "z", axis=0, tiled=True)
+    up, down = [(i, (i + 1) % 8) for i in range(8)], [((i + 1) % 8, i) for i in range(8)]
+
+    def both(lower, upper, *after):
+        lower, upper, *_ = lax.optimization_barrier((lower, upper, *after))
+        return lax.ppermute(lower, "z", up), lax.ppermute(upper, "z", down)
+
 
     across = [(h * 2 + l, (1 - h) * 2 + 1 - l) for h in range(2) for l in range(2)]
     swap, pairs = [(0, 1), (1, 0)], [(0, 1), (1, 0), (2, 3), (3, 2)]
@@ -401,23 +357,43 @@
     queries, _ = lax.optimization_barrier((queries, picked))
     attended, probs = attention_fwd(valid_lengths, queries, keys, values)
     turned = lax.all_to_all(attended, TENSOR, 0, 0, tiled=True)
-    rotated = lax.all_to_all(mix(turned, 1, 1), TENSOR, 0, 0, tiled=True)
+    ring = [both(o_weight, o_weight, attended)]
+    own_blocks = take_own(lax.optimization_barrier((out_grad, attended))[0])
+    mixed = mix(turned, 1, 1)
+    ring.append(both(*ring[0], mixed))
+    rotated = lax.all_to_all(mixed, TENSOR, 0, 0, tiled=True)
     rotated_other = lax.ppermute(rotated, "xh", swap)
-    near, rotated = lax.optimization_barrier((near, rotated))
+    near, tied, *second = lax.optimization_barrier((near, rotated, *ring[1]))
+    ring[1] = tuple(second)
+    ring.append(both(*ring[1]))
     last = lax.ppermute(near[:OVER_Y], "y", pairs)
     far = lax.ppermute(near, "co", swap)
-    own = own_dot(rotated, out_grad)
+    own = own_dot(tied, own_blocks)
     last, far, own = lax.optimization_barrier((last, far, own))
     far_last = lax.ppermute(last, "co", swap)
-    partial, kept = other_dot(rotated_other, own, near, last, far, far_last)
-    summed = lax.psum_scatter(partial, "z", scatter_dimension=0, tiled=True)
-
-    grad_rotated = grad_dot(out_grad, near, far, kept, weights, scale[None, :])
+    rotated_other, *third = lax.optimization_barrier((rotated_other, *ring[2]))
+    ring[2] = tuple(third)
+    ring.append(both(ring[2][0][:HALF], ring[2][1][HALF:]))
+    terms, pieces = other_dot(rotated_other, own, near, last, far, far_last)
+    weights = [o_weight, *ring[0], *ring[1], *ring[2], *ring[3]]
+    grad_rotated = grad_dot(own_blocks, pieces, weights, scale[None, :])
+
+    def add(first, second):
+        return (first.astype(jnp.float32) + second.astype(jnp.float32)).astype(jnp.bfloat16)
+
+    lower, upper = both(terms[4], terms[8])
+    lower = jnp.concatenate([add(lower, terms[3][:HALF]), terms[3][HALF:]])
+    upper = jnp.concatenate([terms[5][:HALF], add(upper, terms[5][HALF:])])
+    lower, upper = both(lower, upper, grad_rotated)
+    lower, upper = both(add(lower, terms[2]), add(upper, terms[6]))
+    lower, upper = both(add(lower, terms[1]), add(upper, terms[7]))
+    summed = lower.astype(jnp.float32) + upper.astype(jnp.float32) + terms[0].astype(jnp.float32)
+
     turned = lax.all_to_all(grad_rotated.reshape(2 * BLK, BLK), ("xh",) + TENSOR, 0, 0, tiled=True)
     grad_attended = lax.all_to_all(mix(turned, 2, 1), TENSOR, 0, 0, tiled=True)
     grad_query, grad_key, grad_value = attention_bwd(probs, queries, keys, values, grad_attended)
 
-    grad_weight = summed.astype(jnp.float32) * scale[:, None]
+    grad_weight = summed * scale[:, None]
     return grad_query, grad_key, grad_value, grad_weight
 
 

time: 140 us -> 137 us (0.979)
  blocking collectives: 66.3 us -> 29.3 us
  starting transfers between devices: 9.41 us -> 42 us
  between operations: 14.9 us -> 1.63 us
  other arithmetic: 2.73 us -> 12.8 us
  waiting for transfers between devices: 10.2 us -> 18.7 us
  Pallas kernels: 31.5 us -> 24.6 us
  local copies, waits for them, and re-layouts: 4.21 us -> 6.68 us
    all_to_all x3 -> x1, blocking collectives: 51.2 us -> 14 us  [body(): rotated = lax.all_to_all(mixed, TENSOR, 0, 0, tiled=True)]
    ppermute x0 -> x16, starting transfers between devices: none -> 23.7 us  [both(): return (lax.ppermute(lower, 'z', up), lax.ppermute(upper, 'z', down))]
    all_to_all x0 -> x2, waiting for transfers between devices: none -> 11.9 us  [the longest x1 7.79 us: body(): lax.all_to_all(grad_rotated.reshape(2 * BLK, BLK), ('xh',) + TENSOR, 0, 0...]
    all_to_all x0 -> x2, starting transfers between devices: none -> 11.6 us  [the longest x1 7.76 us: body(): lax.all_to_all(grad_rotated.reshape(2 * BLK, BLK), ('xh',) + TENSOR, 0, 0...]
    convert_element_type x0 -> x6, other arithmetic: none -> 8.64 us  [add(): (first.astype(jnp.float32) + second.astype(jnp.float32)).astype(jnp.bfloa...]
    pallas_call x3 -> x4, Pallas kernels: 20.1 us -> 12.4 us  [the longest x1 4.52 us: grad_dot(): pl.pallas_call(grad_kernel, in_specs=[VMEM] * 12, out_specs=VMEM, scratch...]
    reduce_scatter x1 -> x0, waiting for transfers between devices: 5.14 us -> none  [body(): summed = lax.psum_scatter(partial, 'z', scatter_dimension=0, tiled=True)]
    ppermute x0 -> x16, waiting for transfers between devices: none -> 4.27 us  [both(): return (lax.ppermute(lower, 'z', up), lax.ppermute(upper, 'z', down))]
  transfers between devices with their start and end apart: 7 -> 23, of which waited for: 4 -> 8; matrix products, arithmetic and copies ran while one was open for 0% -> 7% of each run, Pallas kernels for 23% -> 16%
where the time goes in v4:
time: 137 us; the launch traced here: 136 us
  starting transfers between devices  42 us (31%)
  blocking collectives  29.3 us (21%)
  Pallas kernels  24.6 us (18%)
  waiting for transfers between devices  18.7 us (14%)
  other arithmetic  12.8 us (9%)
  local copies, waits for them, and re-layouts  6.68 us (5%)
  between operations  1.63 us (1%)
    ppermute x16, starting transfers between devices, both(): return (lax.ppermute(lower, 'z', up), lax.ppermute(upper, 'z', down))  23.7 us
    all_to_all x1, blocking collectives, body(): turned = lax.all_to_all(attended, TENSOR, 0, 0, tiled=True)  15.3 us
    all_to_all x1, blocking collectives, body(): rotated = lax.all_to_all(mixed, TENSOR, 0, 0, tiled=True)  14 us
    convert_element_type x6, other arithmetic, add(): (first.astype(jnp.float32) + second.astype(jnp.float32)).astype(jnp.bfloa...  8.64 us
    all_to_all x1, waiting for transfers between devices, body(): lax.all_to_all(grad_rotated.reshape(2 * BLK, BLK), ('xh',) + TENSOR, 0, 0...  7.79 us
    all_to_all x1, starting transfers between devices, body(): lax.all_to_all(grad_rotated.reshape(2 * BLK, BLK), ('xh',) + TENSOR, 0, 0...  7.76 us
    unnamed x32, local copies, waits for them, and re-layouts  6.57 us
    pallas_call x1, Pallas kernels, grad_dot(): pl.pallas_call(grad_kernel, in_specs=[VMEM] * 12, out_specs=VMEM, scratch...  4.52 us
  transfers between devices with their start and end apart: 23, of which 8 were waited for; matrix products, arithmetic and copies ran while one was open for 7% of the time, Pallas kernels for 16%

profile of v4, /device:TPU:1, one launch (start us, length us, event | category | flops | bytes accessed | tf_op | source)
XLA Modules:
  0.0 135.8 jit_solution(6736338427794875088)
XLA Ops:
  0.7 2.7 %pick_units.1 = bf16[6,256,512]{2,1,0:T(8,128)(2,1)} custom-call(bf16[512,8192]{1,0:T(8,128)(2,1)} %grad_ref.2), custom_call_target="tpu_custom_call" | custom-call | tf_op jit(solution)/shard_map/pick_units/pallas_call | solution.py:168
  3.4 3.4 %collective-permute-start.1 = (bf16[6,256,512]{2,1,0:T(8,128)(2,1)}, bf16[6,256,512]{2,1,0:T(8,128)(2,1)S(1)}, u32[]{:S(2)}, u32[]{:S(2)}) collective-permute-start(bf16[6,256,512]{2,1,0:T(8,128)(2,1)} %pick_units.1), channel_id=1, source_target_pairs={{0,18},{2,16},{16,2},{18,0},{1,19},{3,17},{17,3},{19,1},{4,22},{6,... | collective-permute-start | bytes 4718600 | tf_op jit(solution)/shard_map/ppermute | solution.py:355
  7.5 3.5 %attention_fwd.1 = (bf16[512,512]{1,0:T(8,128)(2,1)S(1)}, bf16[4,512,512]{2,1,0:T(8,128)(2,1)S(1)}) custom-call(s32[1]{0:T(128)S(6)} %copy.11.len_ref, bf16[512,512]{1,0:T(8,128)(2,1)S(1)} %copy-done.8, bf16[512,512]{1,0:T(8,128)(2,1)S(1)} %copy-done.10, bf16[512,512]{1,0:T(8,128)(2,1)S(1)} %copy-done.12), custom_call_target="tpu_custom_call" | custom-call | flops 536870912 | bytes 6291456 | tf_op jit(solution)/shard_map/attention_fwd/pallas_call | solution.py:58
  12.6 4.0 %collective-permute-start.3 = (bf16[512,512]{1,0:T(8,128)(2,1)}, bf16[512,512]{1,0:T(8,128)(2,1)S(1)}, u32[]{:S(2)}, u32[]{:S(2)}) collective-permute-start(bf16[512,512]{1,0:T(8,128)(2,1)} %refs_0_.1), channel_id=1, source_target_pairs={{32,0},{64,32},{96,64},{128,96},{160,128},{192,160},{224,192},{0,2... | collective-permute-start | bytes 1572872 | tf_op jit(solution)/shard_map/ppermute | solution.py:348
  16.7 15.3 %all_to_all.45 = bf16[16,32,512]{2,1,0:T(8,128)(2,1)S(1)} all-to-all(bf16[16,32,512]{2,1,0:T(8,128)(2,1)S(1)} %bitcast.16), channel_id=1, replica_groups=mesh['z'=8,'xh'=2,'y'=4,'xl'=2,'co'=2] {'y','xl','co'}, dimensions={0} | all-to-all | bytes 1048576 | tf_op jit(solution)/shard_map/all_to_all | solution.py:359
  32.5 2.7 %collective-permute-start.5 = (bf16[512,512]{1,0:T(8,128)(2,1)S(1)}, bf16[512,512]{1,0:T(8,128)(2,1)S(1)}, u32[]{:S(2)}, u32[]{:S(2)}) collective-permute-start(bf16[512,512]{1,0:T(8,128)(2,1)S(1)} %collective-permute-done.3.refs_2_), channel_id=1, source_target_pairs={{32,0},{64,32},{96,64},{128,96},{160,128},{192,160},{224,192},{0,2... | collective-permute-start | bytes 1572872 | tf_op jit(solution)/shard_map/ppermute | solution.py:348
  35.2 14.0 %all_to_all.46 = bf16[16,32,512]{2,1,0:T(8,128)(2,1)S(1)} all-to-all(bf16[16,32,512]{2,1,0:T(8,128)(2,1)S(1)} %bitcast.12), channel_id=1, replica_groups=mesh['z'=8,'xh'=2,'y'=4,'xl'=2,'co'=2] {'y','xl','co'}, dimensions={0} | all-to-all | bytes 1048576 | tf_op jit(solution)/shard_map/all_to_all | solution.py:364
  51.8 2.7 %collective-permute-start.7 = (bf16[512,512]{1,0:T(8,128)(2,1)S(1)}, bf16[512,512]{1,0:T(8,128)(2,1)S(1)}, u32[]{:S(2)}, u32[]{:S(2)}) collective-permute-start(bf16[512,512]{1,0:T(8,128)(2,1)S(1)} %collective-permute-done.5.refs_4_), channel_id=1, source_target_pairs={{32,0},{64,32},{96,64},{128,96},{160,128},{192,160},{224,192},{0,2... | collective-permute-start | bytes 1572872 | tf_op jit(solution)/shard_map/ppermute | solution.py:348
  54.5 3.4 %copy-done = bf16[512,8192]{1,0:T(8,128)(2,1)S(1)} copy-done((bf16[512,8192]{1,0:T(8,128)(2,1)S(1)}, bf16[512,8192]{1,0:T(8,128)(2,1)}, u32[]{:S(2)}) %copy-start) | copy-done | bytes 8388632
  58.7 3.7 %own_dot.1.own_ref = bf16[8,512,512]{2,1,0:T(8,128)(2,1)S(1)} custom-call(bf16[512,512]{1,0:T(8,128)(2,1)S(1)} %bitcast.11, bf16[8,512,512]{2,1,0:T(8,128)(2,1)S(1)} %take_own.1.own_ref), custom_call_target="tpu_custom_call" | custom-call | flops 2147483648 | bytes 9437184 | tf_op jit(solution)/shard_map/own_dot/pallas_call | solution.py:255
  66.6 2.7 %collective-permute-start.12 = (bf16[256,512]{1,0:T(8,128)(2,1)S(1)}, bf16[256,512]{1,0:T(8,128)(2,1)S(1)}, u32[]{:S(2)}, u32[]{:S(2)}) collective-permute-start(bf16[256,512]{1,0:T(8,128)(2,1)S(1)} %slice.23), channel_id=1, source_target_pairs={{32,0},{64,32},{96,64},{128,96},{160,128},{192,160},{224,192},{0,2... | collective-permute-start | bytes 786440 | tf_op jit(solution)/shard_map/ppermute | solution.py:348
  69.3 3.3 %other_dot.1 = (bf16[512,512]{1,0:T(8,128)(2,1)S(1)}, bf16[512,512]{1,0:T(8,128)(2,1)S(1)}, bf16[512,512]{1,0:T(8,128)(2,1)S(1)}, bf16[512,512]{1,0:T(8,128)(2,1...) custom-call(bf16[512,512]{1,0:T(8,128)(2,1)S(1)} %collective-permute, ...), custom_call_target="tpu_custom_call" | custom-call | flops 2147483648 | bytes 13631488 | tf_op jit(solution)/shard_map/other_dot/pallas_call | solution.py:290
  72.8 2.7 %collective-permute-start.14 = (bf16[256,512]{1,0:T(8,128)(2,1)S(1)}, bf16[256,512]{1,0:T(8,128)(2,1)S(1)}, u32[]{:S(2)}, u32[]{:S(2)}) collective-permute-start(bf16[256,512]{1,0:T(8,128)(2,1)S(1)} %get-tuple-element.78), channel_id=1, source_target_pairs={{32,0},{64,32},{96,64},{128,96},{160,128},{192,160},{224,192},{0,2... | collective-permute-start | bytes 786440 | tf_op jit(solution)/shard_map/ppermute | solution.py:348
  75.5 4.5 %grad_dot.1 = bf16[2,512,512]{2,1,0:T(8,128)(2,1)S(1)} custom-call(bf16[8,512,512]{2,1,0:T(8,128)(2,1)S(1)} %take_own.1.own_ref, bf16[8,512,512]{2,1,0:T(8,128)(2,1)S(1)} %get-tuple-element.65.pieces_ref, f32[1,512]{1,0:T(1,128)S(1)} %bitcast.17, bf16[512,512]{1,0:T(8,128)(2,1)S(1)} %copy-done.14, bf16[512,512]{1,0:T(8,128)(2,1)S(1)} %collective-permute-done.2.refs_1_, ...), custom_call_target="tpu_custom_call" | custom-call | flops 4294967296 | bytes 13631488 | tf_op jit(solution)/shard_map/grad_dot/pallas_call | solution.py:231
  84.7 7.8 %all-to-all-start.2 = ((bf16[32,32,512]{2,1,0:T(8,128)(2,1)}), bf16[32,32,512]{2,1,0:T(8,128)(2,1)S(1)}, u32[]{:S(2)}, u32[]{:S(2)}) async-start(bf16[32,32,512]{2,1,0:T(8,128)(2,1)} %bitcast.15), calls=%async_computation.2 | async-start | bytes 2097152 | tf_op jit(solution)/shard_map/all_to_all | solution.py:392
  96.6 2.1 %add_convert_fusion.2 = bf16[512,512]{1,0:T(8,128)(2,1)} fusion(bf16[512,512]{1,0:T(8,128)(2,1)} %copy-done.4, bf16[512,512]{1,0:T(8,128)(2,1)} %collective-permute-done.16), kind=kLoop, calls=%fused_computation.3 | loop fusion | flops 1048576 | bytes 1572864 | tf_op jit(solution)/shard_map/convert_element_type | solution.py:382
  98.8 2.7 %collective-permute-start.18 = (bf16[512,512]{1,0:T(8,128)(2,1)}, bf16[512,512]{1,0:T(8,128)(2,1)}, u32[]{:S(2)}, u32[]{:S(2)}) collective-permute-start(bf16[512,512]{1,0:T(8,128)(2,1)} %add_convert_fusion.2), channel_id=1, source_target_pairs={{32,0},{64,32},{96,64},{128,96},{160,128},{192,160},{224,192},{0,2... | collective-permute-start | bytes 1572872 | tf_op jit(solution)/shard_map/ppermute | solution.py:348
  101.4 7.8 %all-to-all-done.2 = bf16[32,32,512]{2,1,0:T(8,128)(2,1)S(1)} async-done(((bf16[32,32,512]{2,1,0:T(8,128)(2,1)}), bf16[32,32,512]{2,1,0:T(8,128)(2,1)S(1)}, u32[]{:S(2)}, u32[]{:S(2)}) %all-to-all-start.2) | async-done | bytes 1048608 | tf_op jit(solution)/shard_map/all_to_all | solution.py:392
  110.6 3.9 %all-to-all-start.3 = ((bf16[16,32,512]{2,1,0:T(8,128)(2,1)}), bf16[16,32,512]{2,1,0:T(8,128)(2,1)S(1)}, u32[]{:S(2)}, u32[]{:S(2)}) async-start(bf16[16,32,512]{2,1,0:T(8,128)(2,1)} %bitcast.7), calls=%async_computation.3 | async-start | bytes 1048576 | tf_op jit(solution)/shard_map/all_to_all | solution.py:393
  114.4 2.1 %add_convert_fusion.1 = bf16[512,512]{1,0:T(8,128)(2,1)} fusion(bf16[512,512]{1,0:T(8,128)(2,1)} %copy-done.3, bf16[512,512]{1,0:T(8,128)(2,1)} %collective-permute-done.17), kind=kLoop, calls=%fused_computation.2 | loop fusion | flops 1048576 | bytes 1572864 | tf_op jit(solution)/shard_map/convert_element_type | solution.py:382
  116.6 2.1 %add_convert_fusion = bf16[512,512]{1,0:T(8,128)(2,1)} fusion(bf16[512,512]{1,0:T(8,128)(2,1)} %copy-done.2, bf16[512,512]{1,0:T(8,128)(2,1)} %collective-permute-done.18), kind=kLoop, calls=%fused_computation.1 | loop fusion | flops 1048576 | bytes 1572864 | tf_op jit(solution)/shard_map/convert_element_type | solution.py:382
  120.2 4.2 %all-to-all-done.3 = bf16[16,32,512]{2,1,0:T(8,128)(2,1)S(1)} async-done(((bf16[16,32,512]{2,1,0:T(8,128)(2,1)}), bf16[16,32,512]{2,1,0:T(8,128)(2,1)S(1)}, u32[]{:S(2)}, u32[]{:S(2)}) %all-to-all-start.3) | async-done | bytes 524320 | tf_op jit(solution)/shard_map/all_to_all | solution.py:393
  127.5 4.2 %attention_bwd.1 = (bf16[512,512]{1,0:T(8,128)(2,1)}, bf16[512,512]{1,0:T(8,128)(2,1)}, bf16[512,512]{1,0:T(8,128)(2,1)}) custom-call(bf16[4,512,512]{2,1,0:T(8,128)(2,1)S(1)} %get-tuple-element.48.p_ref, bf16[512,512]{1,0:T(8,128)(2,1)S(1)} %copy-done.9, bf16[512,512]{1,0:T(8,128)(2,1)S(1)} %copy-done.11, bf16[512,512]{1,0:T(8,128)(2,1)S(1)} %copy-done.13, ...), custom_call_target="tpu_custom_call" | custom-call | flops 1073741824 | bytes 6291456 | tf_op jit(solution)/shard_map/attention_bwd/pallas_call | solution.py:95
  133.4 2.4 %add_multiply_fusion = f32[512,512]{1,0:T(8,128)} fusion(bf16[512,512]{1,0:T(8,128)(2,1)S(1)} %copy-done.7, bf16[512,512]{1,0:T(8,128)(2,1)} %collective-permute-done.20, bf16[512,512]{1,0:T(8,128)(2,1)} %collective-permute-done.19, f32[512]{0:T(512)S(1)} %multiply_exponential_fusion), kind=kLoop, calls=%fused_computation | loop fusion | flops 1572864 | bytes 2623488 | tf_op jit(solution)/shard_map/mul | solution.py:396
  (80 shorter events, 26.3 us)
Async XLA Ops:
  3.4 45.9 %collective-permute-start.1 = (bf16[6,256,512]{2,1,0:T(8,128)(2,1)}, bf16[6,256,512]{2,1,0:T(8,128)(2,1)S(1)}, u32[]{:S(2)}, u32[]{:S(2)}) collective-permute-start(bf16[6,256,512]{2,1,0:T(8,128)(2,1)} %pick_units.1), channel_id=1, source_target_pairs={{0,18},{2,16},{16,2},{18,0},{1,19},{3,17},{17,3},{19,1},{4,22},{6,... | collective-permute-start | bytes 4718600 | tf_op jit(solution)/shard_map/ppermute | solution.py:355
  10.9 21.5 %collective-permute-start.2 = (bf16[512,512]{1,0:T(8,128)(2,1)}, bf16[512,512]{1,0:T(8,128)(2,1)S(1)}, u32[]{:S(2)}, u32[]{:S(2)}) collective-permute-start(bf16[512,512]{1,0:T(8,128)(2,1)} %refs_0_.1), channel_id=1, source_target_pairs={{0,32},{32,64},{64,96},{96,128},{128,160},{160,192},{192,224},{224... | collective-permute-start | bytes 1572872 | tf_op jit(solution)/shard_map/ppermute | solution.py:348
  12.6 19.8 %collective-permute-start.3 = (bf16[512,512]{1,0:T(8,128)(2,1)}, bf16[512,512]{1,0:T(8,128)(2,1)S(1)}, u32[]{:S(2)}, u32[]{:S(2)}) collective-permute-start(bf16[512,512]{1,0:T(8,128)(2,1)} %refs_0_.1), channel_id=1, source_target_pairs={{32,0},{64,32},{96,64},{128,96},{160,128},{192,160},{224,192},{0,2... | collective-permute-start | bytes 1572872 | tf_op jit(solution)/shard_map/ppermute | solution.py:348
  32.4 16.8 %collective-permute-start.4 = (bf16[512,512]{1,0:T(8,128)(2,1)S(1)}, bf16[512,512]{1,0:T(8,128)(2,1)S(1)}, u32[]{:S(2)}, u32[]{:S(2)}) collective-permute-start(bf16[512,512]{1,0:T(8,128)(2,1)S(1)} %collective-permute-done.2.refs_1_), channel_id=1, source_target_pairs={{0,32},{32,64},{64,96},{96,128},{128,160},{160,192},{192,224},{224... | collective-permute-start | bytes 1572872 | tf_op jit(solution)/shard_map/ppermute | solution.py:348
  32.5 16.7 %collective-permute-start.5 = (bf16[512,512]{1,0:T(8,128)(2,1)S(1)}, bf16[512,512]{1,0:T(8,128)(2,1)S(1)}, u32[]{:S(2)}, u32[]{:S(2)}) collective-permute-start(bf16[512,512]{1,0:T(8,128)(2,1)S(1)} %collective-permute-done.3.refs_2_), channel_id=1, source_target_pairs={{32,0},{64,32},{96,64},{128,96},{160,128},{192,160},{224,192},{0,2... | collective-permute-start | bytes 1572872 | tf_op jit(solution)/shard_map/ppermute | solution.py:348
  49.2 14.9 %collective-permute-start.9 = (bf16[6,256,512]{2,1,0:T(8,128)(2,1)S(1)}, bf16[6,256,512]{2,1,0:T(8,128)(2,1)S(1)}, u32[]{:S(2)}, u32[]{:S(2)}) collective-permute-start(bf16[6,256,512]{2,1,0:T(8,128)(2,1)S(1)} %collective-permute-done.1.near), channel_id=1, source_target_pairs={{0,1},{1,0},{2,3},{3,2},{4,5},{5,4},{6,7},{7,6},{8,9},{9,8},{10,11... | collective-permute-start | bytes 4718600 | tf_op jit(solution)/shard_map/ppermute | solution.py:370
  50.5 13.6 %collective-permute-start.8 = (bf16[2,256,512]{2,1,0:T(8,128)(2,1)S(1)}, bf16[2,256,512]{2,1,0:T(8,128)(2,1)S(1)}, u32[]{:S(2)}, u32[]{:S(2)}) collective-permute-start(bf16[2,256,512]{2,1,0:T(8,128)(2,1)S(1)} %slice.21), channel_id=1, source_target_pairs={{0,4},{4,0},{8,12},{12,8},{1,5},{5,1},{9,13},{13,9},{2,6},{6,2},{1... | collective-permute-start | bytes 1572872 | tf_op jit(solution)/shard_map/ppermute | solution.py:369
  50.6 15.1 %collective-permute-start = (bf16[512,512]{1,0:T(8,128)(2,1)S(1)}, bf16[512,512]{1,0:T(8,128)(2,1)S(1)}, u32[]{:S(2)}, u32[]{:S(2)}) collective-permute-start(bf16[512,512]{1,0:T(8,128)(2,1)S(1)} %bitcast.10), channel_id=1, source_target_pairs={{0,16},{16,0},{1,17},{17,1},{2,18},{18,2},{3,19},{19,3},{4,20},{20... | collective-permute-start | bytes 1572872 | tf_op jit(solution)/shard_map/ppermute | solution.py:365
  51.8 14.4 %collective-permute-start.6 = (bf16[512,512]{1,0:T(8,128)(2,1)S(1)}, bf16[512,512]{1,0:T(8,128)(2,1)S(1)}, u32[]{:S(2)}, u32[]{:S(2)}) collective-permute-start(bf16[512,512]{1,0:T(8,128)(2,1)S(1)} %collective-permute-done.4.refs_3_), channel_id=1, source_target_pairs={{0,32},{32,64},{64,96},{96,128},{128,160},{160,192},{192,224},{224... | collective-permute-start | bytes 1572872 | tf_op jit(solution)/shard_map/ppermute | solution.py:348
  51.8 14.4 %collective-permute-start.7 = (bf16[512,512]{1,0:T(8,128)(2,1)S(1)}, bf16[512,512]{1,0:T(8,128)(2,1)S(1)}, u32[]{:S(2)}, u32[]{:S(2)}) collective-permute-start(bf16[512,512]{1,0:T(8,128)(2,1)S(1)} %collective-permute-done.5.refs_4_), channel_id=1, source_target_pairs={{32,0},{64,32},{96,64},{128,96},{160,128},{192,160},{224,192},{0,2... | collective-permute-start | bytes 1572872 | tf_op jit(solution)/shard_map/ppermute | solution.py:348
  64.2 5.1 %collective-permute-start.10 = (bf16[2,256,512]{2,1,0:T(8,128)(2,1)S(1)}, bf16[2,256,512]{2,1,0:T(8,128)(2,1)S(1)}, u32[]{:S(2)}, u32[]{:S(2)}) collective-permute-start(bf16[2,256,512]{2,1,0:T(8,128)(2,1)S(1)} %collective-permute-done.8.last), channel_id=1, source_target_pairs={{0,1},{1,0},{2,3},{3,2},{4,5},{5,4},{6,7},{7,6},{8,9},{9,8},{10,11... | collective-permute-start | bytes 1572872 | tf_op jit(solution)/shard_map/ppermute | solution.py:373
  66.3 9.2 %collective-permute-start.11 = (bf16[256,512]{1,0:T(8,128)(2,1)S(1)}, bf16[256,512]{1,0:T(8,128)(2,1)S(1)}, u32[]{:S(2)}, u32[]{:S(2)}) collective-permute-start(bf16[256,512]{1,0:T(8,128)(2,1)S(1)} %slice.22), channel_id=1, source_target_pairs={{0,32},{32,64},{64,96},{96,128},{128,160},{160,192},{192,224},{224... | collective-permute-start | bytes 786440 | tf_op jit(solution)/shard_map/ppermute | solution.py:348
  66.6 8.9 %collective-permute-start.12 = (bf16[256,512]{1,0:T(8,128)(2,1)S(1)}, bf16[256,512]{1,0:T(8,128)(2,1)S(1)}, u32[]{:S(2)}, u32[]{:S(2)}) collective-permute-start(bf16[256,512]{1,0:T(8,128)(2,1)S(1)} %slice.23), channel_id=1, source_target_pairs={{32,0},{64,32},{96,64},{128,96},{160,128},{192,160},{224,192},{0,2... | collective-permute-start | bytes 786440 | tf_op jit(solution)/shard_map/ppermute | solution.py:348
  72.7 7.4 %collective-permute-start.13 = (bf16[256,512]{1,0:T(8,128)(2,1)S(1)}, bf16[256,512]{1,0:T(8,128)(2,1)S(1)}, u32[]{:S(2)}, u32[]{:S(2)}) collective-permute-start(bf16[256,512]{1,0:T(8,128)(2,1)S(1)} %get-tuple-element.75), channel_id=1, source_target_pairs={{0,32},{32,64},{64,96},{96,128},{128,160},{160,192},{192,224},{224... | collective-permute-start | bytes 786440 | tf_op jit(solution)/shard_map/ppermute | solution.py:348
  72.8 8.3 %collective-permute-start.14 = (bf16[256,512]{1,0:T(8,128)(2,1)S(1)}, bf16[256,512]{1,0:T(8,128)(2,1)S(1)}, u32[]{:S(2)}, u32[]{:S(2)}) collective-permute-start(bf16[256,512]{1,0:T(8,128)(2,1)S(1)} %get-tuple-element.78), channel_id=1, source_target_pairs={{32,0},{64,32},{96,64},{128,96},{160,128},{192,160},{224,192},{0,2... | collective-permute-start | bytes 786440 | tf_op jit(solution)/shard_map/ppermute | solution.py:348
  82.0 12.5 %collective-permute-start.15 = (bf16[512,512]{1,0:T(8,128)(2,1)}, bf16[512,512]{1,0:T(8,128)(2,1)}, u32[]{:S(2)}, u32[]{:S(2)}) collective-permute-start(bf16[512,512]{1,0:T(8,128)(2,1)} %pad_maximum_fusion), channel_id=1, source_target_pairs={{0,32},{32,64},{64,96},{96,128},{128,160},{160,192},{192,224},{224... | collective-permute-start | bytes 1572872 | tf_op jit(solution)/shard_map/ppermute | solution.py:348
  82.8 13.9 %collective-permute-start.16 = (bf16[512,512]{1,0:T(8,128)(2,1)}, bf16[512,512]{1,0:T(8,128)(2,1)}, u32[]{:S(2)}, u32[]{:S(2)}) collective-permute-start(bf16[512,512]{1,0:T(8,128)(2,1)} %pad_maximum_fusion.1), channel_id=1, source_target_pairs={{32,0},{64,32},{96,64},{128,96},{160,128},{192,160},{224,192},{0,2... | collective-permute-start | bytes 1572872 | tf_op jit(solution)/shard_map/ppermute | solution.py:348
  84.7 24.5 %all-to-all-start.2 = ((bf16[32,32,512]{2,1,0:T(8,128)(2,1)}), bf16[32,32,512]{2,1,0:T(8,128)(2,1)S(1)}, u32[]{:S(2)}, u32[]{:S(2)}) async-start(bf16[32,32,512]{2,1,0:T(8,128)(2,1)} %bitcast.15), calls=%async_computation.2 | async-start | bytes 2097152 | tf_op jit(solution)/shard_map/all_to_all | solution.py:392
  98.7 15.7 %collective-permute-start.17 = (bf16[512,512]{1,0:T(8,128)(2,1)}, bf16[512,512]{1,0:T(8,128)(2,1)}, u32[]{:S(2)}, u32[]{:S(2)}) collective-permute-start(bf16[512,512]{1,0:T(8,128)(2,1)} %add_convert_fusion.3), channel_id=1, source_target_pairs={{0,32},{32,64},{64,96},{96,128},{128,160},{160,192},{192,224},{224... | collective-permute-start | bytes 1572872 | tf_op jit(solution)/shard_map/ppermute | solution.py:348
  98.8 17.8 %collective-permute-start.18 = (bf16[512,512]{1,0:T(8,128)(2,1)}, bf16[512,512]{1,0:T(8,128)(2,1)}, u32[]{:S(2)}, u32[]{:S(2)}) collective-permute-start(bf16[512,512]{1,0:T(8,128)(2,1)} %add_convert_fusion.2), channel_id=1, source_target_pairs={{32,0},{64,32},{96,64},{128,96},{160,128},{192,160},{224,192},{0,2... | collective-permute-start | bytes 1572872 | tf_op jit(solution)/shard_map/ppermute | solution.py:348
  110.6 22.8 %copy-start.7 = (bf16[512,512]{1,0:T(8,128)(2,1)S(1)}, bf16[512,512]{1,0:T(8,128)(2,1)}, u32[]{:S(2)}) copy-start(bf16[512,512]{1,0:T(8,128)(2,1)} %copy-done.6) | copy-start | bytes 1572868
  110.6 13.8 %all-to-all-start.3 = ((bf16[16,32,512]{2,1,0:T(8,128)(2,1)}), bf16[16,32,512]{2,1,0:T(8,128)(2,1)S(1)}, u32[]{:S(2)}, u32[]{:S(2)}) async-start(bf16[16,32,512]{2,1,0:T(8,128)(2,1)} %bitcast.7), calls=%async_computation.3 | async-start | bytes 1048576 | tf_op jit(solution)/shard_map/all_to_all | solution.py:393
  118.7 13.4 %collective-permute-start.20 = (bf16[512,512]{1,0:T(8,128)(2,1)}, bf16[512,512]{1,0:T(8,128)(2,1)}, u32[]{:S(2)}, u32[]{:S(2)}) collective-permute-start(bf16[512,512]{1,0:T(8,128)(2,1)} %add_convert_fusion), channel_id=1, source_target_pairs={{32,0},{64,32},{96,64},{128,96},{160,128},{192,160},{224,192},{0,2... | collective-permute-start | bytes 1572872 | tf_op jit(solution)/shard_map/ppermute | solution.py:348
  119.1 14.3 %collective-permute-start.19 = (bf16[512,512]{1,0:T(8,128)(2,1)}, bf16[512,512]{1,0:T(8,128)(2,1)}, u32[]{:S(2)}, u32[]{:S(2)}) collective-permute-start(bf16[512,512]{1,0:T(8,128)(2,1)} %add_convert_fusion.1), channel_id=1, source_target_pairs={{0,32},{32,64},{64,96},{96,128},{128,160},{160,192},{192,224},{224... | collective-permute-start | bytes 1572872 | tf_op jit(solution)/shard_map/ppermute | solution.py:348
  (15 other events, 85.4 us)

commit v5 on v4

--- a/solution.py
+++ b/solution.py
@@ -106,7 +106,7 @@
 
 
 def unit_of(v, y_bit):
-    return jnp.where(y_bit == 0, v, 7 - v)
+    return jnp.where(y_bit == 0, v, 6 - 2 * (v // 2) + lax.rem(v, 2))
 
 
 def block_of(i, p):
@@ -131,7 +131,8 @@
 
         each(0, OVER_X, begin)
         for w in range(OVER_Y):
-            pltpu.make_async_copy(over_y.at[w], target(group, 7 - w), sems.at[8 * group + 7 - w]).start()
+            v = OVER_X + w
+            pltpu.make_async_copy(over_y.at[w], target(group, v), sems.at[8 * group + v]).start()
 
     def wait(i):
         group = i // 4
@@ -151,29 +152,14 @@
     lax.fori_loop(first, first + count, body, 0)
 
 
-def pick_kernel(grad_ref, out_ref, sems):
+def pick_units(out_grad):
     x_hi, core, y_bit = place_here()
 
-    def copy(v):
-        unit = unit_of(v, y_bit)
-        rows = pl.ds(pl.multiple_of(lax.rem(unit, 2) * HALF, HALF), HALF)
-        column = pl.multiple_of((2 * (4 * core + unit // 2) + 1 - x_hi) * BLK, BLK)
-        return pltpu.make_async_copy(grad_ref.at[rows, pl.ds(column, BLK)], out_ref.at[v], sems.at[v])
-
-    each(0, OVER_X, lambda v: copy(v).start())
-    each(0, OVER_X, lambda v: copy(v).wait())
-
-
-def pick_units(out_grad):
-    return pl.pallas_call(
-        pick_kernel,
-        in_specs=[HBM],
-        out_specs=VMEM,
-        scratch_shapes=[pltpu.SemaphoreType.DMA((OVER_X,))],
-        out_shape=jax.ShapeDtypeStruct((OVER_X, HALF, BLK), jnp.bfloat16),
-        compiler_params=params(60),
-        name="pick_units",
-    )(out_grad)
+    def block(j):
+        column = (2 * (4 * core + jnp.where(y_bit == 0, j, 3 - j)) + 1 - x_hi) * BLK
+        return lax.dynamic_slice(out_grad, (0, column), (BLK, BLK))
+
+    return jnp.stack([block(j) for j in range(OVER_X // 2)]).reshape(OVER_X, HALF, BLK)
 
 
 def take_kernel(grad_ref, out_ref, sems):

time: 137 us -> 137 us (level)
  waiting for transfers between devices: 18.7 us -> 22.5 us
  Pallas kernels: 24.6 us -> 22.1 us
    ppermute x1, waiting for transfers between devices: 1.73 us -> 5.17 us  [body(): last = lax.ppermute(near[:OVER_Y], 'y', pairs)]
    pallas_call x1 -> x0, Pallas kernels: 2.71 us -> none  [pick_units(): pl.pallas_call(pick_kernel, in_specs=[HBM], out_specs=VMEM, scratch_shape...]
    unnamed x32 -> x36, local copies, waits for them, and re-layouts: 6.57 us -> 3.99 us
    another operation x0 -> x1, local copies, waits for them, and re-layouts: none -> 1.59 us  [pick_units(): jnp.stack([block(j) for j in range(OVER_X // 2)]).reshape(OVER_X, HALF, BLK)]
where the time goes in v5:
time: 137 us; the launch traced here: 136 us
  starting transfers between devices  42.3 us (31%)
  blocking collectives  29.7 us (22%)
  waiting for transfers between devices  22.5 us (16%)
  Pallas kernels  22.1 us (16%)
  other arithmetic  12.5 us (9%)
  local copies, waits for them, and re-layouts  5.69 us (4%)
  between operations  1.64 us (1%)
    ppermute x16, starting transfers between devices, both(): return (lax.ppermute(lower, 'z', up), lax.ppermute(upper, 'z', down))  23.7 us
    all_to_all x1, blocking collectives, body(): turned = lax.all_to_all(attended, TENSOR, 0, 0, tiled=True)  15.7 us
    all_to_all x1, blocking collectives, body(): rotated = lax.all_to_all(mixed, TENSOR, 0, 0, tiled=True)  14 us
    convert_element_type x6, other arithmetic, add(): (first.astype(jnp.float32) + second.astype(jnp.float32)).astype(jnp.bfloa...  8.33 us
    all_to_all x1, waiting for transfers between devices, body(): lax.all_to_all(grad_rotated.reshape(2 * BLK, BLK), ('xh',) + TENSOR, 0, 0...  8.08 us
    all_to_all x1, starting transfers between devices, body(): lax.all_to_all(grad_rotated.reshape(2 * BLK, BLK), ('xh',) + TENSOR, 0, 0...  7.88 us
    ppermute x1, waiting for transfers between devices, body(): last = lax.ppermute(near[:OVER_Y], 'y', pairs)  5.17 us
    pallas_call x1, Pallas kernels, grad_dot(): pl.pallas_call(grad_kernel, in_specs=[VMEM] * 12, out_specs=VMEM, scratch...  4.52 us
  transfers between devices with their start and end apart: 23, of which 8 were waited for; matrix products, arithmetic and copies ran while one was open for 7% of the time, Pallas kernels for 16%

profile of v5, /device:TPU:1, one launch (start us, length us, event | category | flops | bytes accessed | tf_op | source)
XLA Modules:
  0.0 136.4 jit_solution(9927715211247580441)
XLA Ops:
  2.5 3.4 %collective-permute-start.1 = (bf16[6,256,512]{2,1,0:T(8,128)(2,1)S(1)}, bf16[6,256,512]{2,1,0:T(8,128)(2,1)S(1)}, u32[]{:S(2)}, u32[]{:S(2)}) collective-permute-start(bf16[6,256,512]{2,1,0:T(8,128)(2,1)S(1)} %bitcast.25), channel_id=1, source_target_pairs={{0,18},{2,16},{16,2},{18,0},{1,19},{3,17},{17,3},{19,1},{4,22},{6,... | collective-permute-start | bytes 4718600 | tf_op jit(solution)/shard_map/ppermute | solution.py:341
  6.6 3.5 %attention_fwd.1 = (bf16[512,512]{1,0:T(8,128)(2,1)S(1)}, bf16[4,512,512]{2,1,0:T(8,128)(2,1)S(1)}) custom-call(s32[1]{0:T(128)S(6)} %copy.11.len_ref, bf16[512,512]{1,0:T(8,128)(2,1)S(1)} %copy-done.10, bf16[512,512]{1,0:T(8,128)(2,1)S(1)} %copy-done.12, bf16[512,512]{1,0:T(8,128)(2,1)S(1)} %copy-done.14), custom_call_target="tpu_custom_call" | custom-call | flops 536870912 | bytes 6291456 | tf_op jit(solution)/shard_map/attention_fwd/pallas_call | solution.py:58
  11.8 4.0 %collective-permute-start.3 = (bf16[512,512]{1,0:T(8,128)(2,1)S(1)}, bf16[512,512]{1,0:T(8,128)(2,1)S(1)}, u32[]{:S(2)}, u32[]{:S(2)}) collective-permute-start(bf16[512,512]{1,0:T(8,128)(2,1)S(1)} %copy-done.16), channel_id=1, source_target_pairs={{32,0},{64,32},{96,64},{128,96},{160,128},{192,160},{224,192},{0,2... | collective-permute-start | bytes 1572872 | tf_op jit(solution)/shard_map/ppermute | solution.py:334
  15.8 15.7 %all_to_all.45 = bf16[16,32,512]{2,1,0:T(8,128)(2,1)S(1)} all-to-all(bf16[16,32,512]{2,1,0:T(8,128)(2,1)S(1)} %bitcast.23), channel_id=1, replica_groups=mesh['z'=8,'xh'=2,'y'=4,'xl'=2,'co'=2] {'y','xl','co'}, dimensions={0} | all-to-all | bytes 1048576 | tf_op jit(solution)/shard_map/all_to_all | solution.py:345
  32.0 2.7 %collective-permute-start.5 = (bf16[512,512]{1,0:T(8,128)(2,1)S(1)}, bf16[512,512]{1,0:T(8,128)(2,1)S(1)}, u32[]{:S(2)}, u32[]{:S(2)}) collective-permute-start(bf16[512,512]{1,0:T(8,128)(2,1)S(1)} %collective-permute-done.3.refs_2_), channel_id=1, source_target_pairs={{32,0},{64,32},{96,64},{128,96},{160,128},{192,160},{224,192},{0,2... | collective-permute-start | bytes 1572872 | tf_op jit(solution)/shard_map/ppermute | solution.py:334
  34.7 14.0 %all_to_all.46 = bf16[16,32,512]{2,1,0:T(8,128)(2,1)S(1)} all-to-all(bf16[16,32,512]{2,1,0:T(8,128)(2,1)S(1)} %bitcast.19), channel_id=1, replica_groups=mesh['z'=8,'xh'=2,'y'=4,'xl'=2,'co'=2] {'y','xl','co'}, dimensions={0} | all-to-all | bytes 1048576 | tf_op jit(solution)/shard_map/all_to_all | solution.py:350
  51.3 2.7 %collective-permute-start.7 = (bf16[512,512]{1,0:T(8,128)(2,1)S(1)}, bf16[512,512]{1,0:T(8,128)(2,1)S(1)}, u32[]{:S(2)}, u32[]{:S(2)}) collective-permute-start(bf16[512,512]{1,0:T(8,128)(2,1)S(1)} %collective-permute-done.5.refs_4_), channel_id=1, source_target_pairs={{32,0},{64,32},{96,64},{128,96},{160,128},{192,160},{224,192},{0,2... | collective-permute-start | bytes 1572872 | tf_op jit(solution)/shard_map/ppermute | solution.py:334
  54.7 3.8 %own_dot.1.own_ref = bf16[8,512,512]{2,1,0:T(8,128)(2,1)S(1)} custom-call(bf16[512,512]{1,0:T(8,128)(2,1)S(1)} %bitcast.18, bf16[8,512,512]{2,1,0:T(8,128)(2,1)S(1)} %take_own.1.own_ref), custom_call_target="tpu_custom_call" | custom-call | flops 2147483648 | bytes 9437184 | tf_op jit(solution)/shard_map/own_dot/pallas_call | solution.py:241
  58.5 5.2 %collective-permute-done.8.last = bf16[2,256,512]{2,1,0:T(8,128)(2,1)S(1)} collective-permute-done((bf16[2,256,512]{2,1,0:T(8,128)(2,1)S(1)}, bf16[2,256,512]{2,1,0:T(8,128)(2,1)S(1)}, u32[]{:S(2)}, u32[]{:S(2)}) %collective-permute-start.8) | collective-permute-done | bytes 524320 | tf_op jit(solution)/shard_map/ppermute | solution.py:355
  66.0 2.7 %collective-permute-start.12 = (bf16[256,512]{1,0:T(8,128)(2,1)S(1)}, bf16[256,512]{1,0:T(8,128)(2,1)S(1)}, u32[]{:S(2)}, u32[]{:S(2)}) collective-permute-start(bf16[256,512]{1,0:T(8,128)(2,1)S(1)} %slice.23), channel_id=1, source_target_pairs={{32,0},{64,32},{96,64},{128,96},{160,128},{192,160},{224,192},{0,2... | collective-permute-start | bytes 786440 | tf_op jit(solution)/shard_map/ppermute | solution.py:334
  68.7 3.5 %other_dot.1 = (bf16[512,512]{1,0:T(8,128)(2,1)S(1)}, bf16[512,512]{1,0:T(8,128)(2,1)S(1)}, bf16[512,512]{1,0:T(8,128)(2,1)S(1)}, bf16[512,512]{1,0:T(8,128)(2,1...) custom-call(bf16[512,512]{1,0:T(8,128)(2,1)S(1)} %collective-permute, ...), custom_call_target="tpu_custom_call" | custom-call | flops 2147483648 | bytes 13631488 | tf_op jit(solution)/shard_map/other_dot/pallas_call | solution.py:276
  73.1 2.7 %collective-permute-start.14 = (bf16[256,512]{1,0:T(8,128)(2,1)S(1)}, bf16[256,512]{1,0:T(8,128)(2,1)S(1)}, u32[]{:S(2)}, u32[]{:S(2)}) collective-permute-start(bf16[256,512]{1,0:T(8,128)(2,1)S(1)} %get-tuple-element.78), channel_id=1, source_target_pairs={{32,0},{64,32},{96,64},{128,96},{160,128},{192,160},{224,192},{0,2... | collective-permute-start | bytes 786440 | tf_op jit(solution)/shard_map/ppermute | solution.py:334
  75.8 4.5 %grad_dot.1 = bf16[2,512,512]{2,1,0:T(8,128)(2,1)S(1)} custom-call(bf16[8,512,512]{2,1,0:T(8,128)(2,1)S(1)} %take_own.1.own_ref, bf16[8,512,512]{2,1,0:T(8,128)(2,1)S(1)} %get-tuple-element.65.pieces_ref, f32[1,512]{1,0:T(1,128)S(1)} %bitcast.24, bf16[512,512]{1,0:T(8,128)(2,1)S(1)} %copy-done.16, bf16[512,512]{1,0:T(8,128)(2,1)S(1)} %collective-permute-done.2.refs_1_, ...), custom_call_target="tpu_custom_call" | custom-call | flops 4294967296 | bytes 13631488 | tf_op jit(solution)/shard_map/grad_dot/pallas_call | solution.py:217
  82.4 2.7 %collective-permute-start.16 = (bf16[512,512]{1,0:T(8,128)(2,1)}, bf16[512,512]{1,0:T(8,128)(2,1)}, u32[]{:S(2)}, u32[]{:S(2)}) collective-permute-start(bf16[512,512]{1,0:T(8,128)(2,1)} %pad_maximum_fusion.2), channel_id=1, source_target_pairs={{32,0},{64,32},{96,64},{128,96},{160,128},{192,160},{224,192},{0,2... | collective-permute-start | bytes 1572872 | tf_op jit(solution)/shard_map/ppermute | solution.py:334
  85.0 7.9 %all-to-all-start.2 = ((bf16[32,32,512]{2,1,0:T(8,128)(2,1)}), bf16[32,32,512]{2,1,0:T(8,128)(2,1)S(1)}, u32[]{:S(2)}, u32[]{:S(2)}) async-start(bf16[32,32,512]{2,1,0:T(8,128)(2,1)} %bitcast.22), calls=%async_computation.2 | async-start | bytes 2097152 | tf_op jit(solution)/shard_map/all_to_all | solution.py:378
  94.8 2.1 %add_convert_fusion.3 = bf16[512,512]{1,0:T(8,128)(2,1)} fusion(bf16[512,512]{1,0:T(8,128)(2,1)} %copy-done.7, bf16[512,512]{1,0:T(8,128)(2,1)} %collective-permute-done.15), kind=kLoop, calls=%fused_computation.5 | loop fusion | flops 1048576 | bytes 1572864 | tf_op jit(solution)/shard_map/convert_element_type | solution.py:368
  97.0 2.0 %add_convert_fusion.2 = bf16[512,512]{1,0:T(8,128)(2,1)} fusion(bf16[512,512]{1,0:T(8,128)(2,1)S(1)} %copy-done.6, bf16[512,512]{1,0:T(8,128)(2,1)} %collective-permute-done.16), kind=kLoop, calls=%fused_computation.4 | loop fusion | flops 1048576 | bytes 1572864 | tf_op jit(solution)/shard_map/convert_element_type | solution.py:368
  98.9 2.7 %collective-permute-start.18 = (bf16[512,512]{1,0:T(8,128)(2,1)}, bf16[512,512]{1,0:T(8,128)(2,1)}, u32[]{:S(2)}, u32[]{:S(2)}) collective-permute-start(bf16[512,512]{1,0:T(8,128)(2,1)} %add_convert_fusion.2), channel_id=1, source_target_pairs={{32,0},{64,32},{96,64},{128,96},{160,128},{192,160},{224,192},{0,2... | collective-permute-start | bytes 1572872 | tf_op jit(solution)/shard_map/ppermute | solution.py:334
  101.6 8.1 %all-to-all-done.2 = bf16[32,32,512]{2,1,0:T(8,128)(2,1)S(1)} async-done(((bf16[32,32,512]{2,1,0:T(8,128)(2,1)}), bf16[32,32,512]{2,1,0:T(8,128)(2,1)S(1)}, u32[]{:S(2)}, u32[]{:S(2)}) %all-to-all-start.2) | async-done | bytes 1048608 | tf_op jit(solution)/shard_map/all_to_all | solution.py:378
  111.0 4.1 %all-to-all-start.3 = ((bf16[16,32,512]{2,1,0:T(8,128)(2,1)}), bf16[16,32,512]{2,1,0:T(8,128)(2,1)S(1)}, u32[]{:S(2)}, u32[]{:S(2)}) async-start(bf16[16,32,512]{2,1,0:T(8,128)(2,1)} %bitcast.11), calls=%async_computation.3 | async-start | bytes 1048576 | tf_op jit(solution)/shard_map/all_to_all | solution.py:379
  115.1 2.1 %add_convert_fusion.1 = bf16[512,512]{1,0:T(8,128)(2,1)} fusion(bf16[512,512]{1,0:T(8,128)(2,1)} %copy-done.4, bf16[512,512]{1,0:T(8,128)(2,1)} %collective-permute-done.17), kind=kLoop, calls=%fused_computation.3 | loop fusion | flops 1048576 | bytes 1572864 | tf_op jit(solution)/shard_map/convert_element_type | solution.py:368
  120.7 4.3 %all-to-all-done.3 = bf16[16,32,512]{2,1,0:T(8,128)(2,1)S(1)} async-done(((bf16[16,32,512]{2,1,0:T(8,128)(2,1)}), bf16[16,32,512]{2,1,0:T(8,128)(2,1)S(1)}, u32[]{:S(2)}, u32[]{:S(2)}) %all-to-all-start.3) | async-done | bytes 524320 | tf_op jit(solution)/shard_map/all_to_all | solution.py:379
  128.1 4.2 %attention_bwd.1 = (bf16[512,512]{1,0:T(8,128)(2,1)}, bf16[512,512]{1,0:T(8,128)(2,1)}, bf16[512,512]{1,0:T(8,128)(2,1)}) custom-call(bf16[4,512,512]{2,1,0:T(8,128)(2,1)S(1)} %get-tuple-element.48.p_ref, bf16[512,512]{1,0:T(8,128)(2,1)S(1)} %copy-done.11, bf16[512,512]{1,0:T(8,128)(2,1)S(1)} %copy-done.13, bf16[512,512]{1,0:T(8,128)(2,1)S(1)} %copy-done.15, ...), custom_call_target="tpu_custom_call" | custom-call | flops 1073741824 | bytes 6291456 | tf_op jit(solution)/shard_map/attention_bwd/pallas_call | solution.py:95
  134.1 2.2 %add_multiply_fusion = f32[512,512]{1,0:T(8,128)} fusion(bf16[512,512]{1,0:T(8,128)(2,1)S(1)} %copy-done.9, bf16[512,512]{1,0:T(8,128)(2,1)S(1)} %collective-permute-done.20, bf16[512,512]{1,0:T(8,128)(2,1)} %collective-permute-done.19, f32[512]{0:T(512)S(1)} %multiply_exponential_fusion), kind=kLoop, calls=%fused_computation.1 | loop fusion | flops 1572864 | bytes 2623488 | tf_op jit(solution)/shard_map/mul | solution.py:382
  (85 shorter events, 24.1 us)
Async XLA Ops:
  2.3 51.6 %copy-start = (bf16[512,8192]{1,0:T(8,128)(2,1)S(1)}, bf16[512,8192]{1,0:T(8,128)(2,1)}, u32[]{:S(2)}) copy-start(bf16[512,8192]{1,0:T(8,128)(2,1)} %grad_ref) | copy-start | bytes 25165828
  2.5 46.3 %collective-permute-start.1 = (bf16[6,256,512]{2,1,0:T(8,128)(2,1)S(1)}, bf16[6,256,512]{2,1,0:T(8,128)(2,1)S(1)}, u32[]{:S(2)}, u32[]{:S(2)}) collective-permute-start(bf16[6,256,512]{2,1,0:T(8,128)(2,1)S(1)} %bitcast.25), channel_id=1, source_target_pairs={{0,18},{2,16},{16,2},{18,0},{1,19},{3,17},{17,3},{19,1},{4,22},{6,... | collective-permute-start | bytes 4718600 | tf_op jit(solution)/shard_map/ppermute | solution.py:341
  10.0 21.9 %collective-permute-start.2 = (bf16[512,512]{1,0:T(8,128)(2,1)S(1)}, bf16[512,512]{1,0:T(8,128)(2,1)S(1)}, u32[]{:S(2)}, u32[]{:S(2)}) collective-permute-start(bf16[512,512]{1,0:T(8,128)(2,1)S(1)} %copy-done.16), channel_id=1, source_target_pairs={{0,32},{32,64},{64,96},{96,128},{128,160},{160,192},{192,224},{224... | collective-permute-start | bytes 1572872 | tf_op jit(solution)/shard_map/ppermute | solution.py:334
  11.8 20.2 %collective-permute-start.3 = (bf16[512,512]{1,0:T(8,128)(2,1)S(1)}, bf16[512,512]{1,0:T(8,128)(2,1)S(1)}, u32[]{:S(2)}, u32[]{:S(2)}) collective-permute-start(bf16[512,512]{1,0:T(8,128)(2,1)S(1)} %copy-done.16), channel_id=1, source_target_pairs={{32,0},{64,32},{96,64},{128,96},{160,128},{192,160},{224,192},{0,2... | collective-permute-start | bytes 1572872 | tf_op jit(solution)/shard_map/ppermute | solution.py:334
  31.9 16.8 %collective-permute-start.4 = (bf16[512,512]{1,0:T(8,128)(2,1)S(1)}, bf16[512,512]{1,0:T(8,128)(2,1)S(1)}, u32[]{:S(2)}, u32[]{:S(2)}) collective-permute-start(bf16[512,512]{1,0:T(8,128)(2,1)S(1)} %collective-permute-done.2.refs_1_), channel_id=1, source_target_pairs={{0,32},{32,64},{64,96},{96,128},{128,160},{160,192},{192,224},{224... | collective-permute-start | bytes 1572872 | tf_op jit(solution)/shard_map/ppermute | solution.py:334
  32.0 16.7 %collective-permute-start.5 = (bf16[512,512]{1,0:T(8,128)(2,1)S(1)}, bf16[512,512]{1,0:T(8,128)(2,1)S(1)}, u32[]{:S(2)}, u32[]{:S(2)}) collective-permute-start(bf16[512,512]{1,0:T(8,128)(2,1)S(1)} %collective-permute-done.3.refs_2_), channel_id=1, source_target_pairs={{32,0},{64,32},{96,64},{128,96},{160,128},{192,160},{224,192},{0,2... | collective-permute-start | bytes 1572872 | tf_op jit(solution)/shard_map/ppermute | solution.py:334
  48.7 14.9 %collective-permute-start.9 = (bf16[6,256,512]{2,1,0:T(8,128)(2,1)S(1)}, bf16[6,256,512]{2,1,0:T(8,128)(2,1)S(1)}, u32[]{:S(2)}, u32[]{:S(2)}) collective-permute-start(bf16[6,256,512]{2,1,0:T(8,128)(2,1)S(1)} %collective-permute-done.1.near), channel_id=1, source_target_pairs={{0,1},{1,0},{2,3},{3,2},{4,5},{5,4},{6,7},{7,6},{8,9},{9,8},{10,11... | collective-permute-start | bytes 4718600 | tf_op jit(solution)/shard_map/ppermute | solution.py:356
  50.0 13.6 %collective-permute-start.8 = (bf16[2,256,512]{2,1,0:T(8,128)(2,1)S(1)}, bf16[2,256,512]{2,1,0:T(8,128)(2,1)S(1)}, u32[]{:S(2)}, u32[]{:S(2)}) collective-permute-start(bf16[2,256,512]{2,1,0:T(8,128)(2,1)S(1)} %slice.21), channel_id=1, source_target_pairs={{0,4},{4,0},{8,12},{12,8},{1,5},{5,1},{9,13},{13,9},{2,6},{6,2},{1... | collective-permute-start | bytes 1572872 | tf_op jit(solution)/shard_map/ppermute | solution.py:355
  50.1 15.1 %collective-permute-start = (bf16[512,512]{1,0:T(8,128)(2,1)S(1)}, bf16[512,512]{1,0:T(8,128)(2,1)S(1)}, u32[]{:S(2)}, u32[]{:S(2)}) collective-permute-start(bf16[512,512]{1,0:T(8,128)(2,1)S(1)} %bitcast.17), channel_id=1, source_target_pairs={{0,16},{16,0},{1,17},{17,1},{2,18},{18,2},{3,19},{19,3},{4,20},{20... | collective-permute-start | bytes 1572872 | tf_op jit(solution)/shard_map/ppermute | solution.py:351
  51.3 14.4 %collective-permute-start.6 = (bf16[512,512]{1,0:T(8,128)(2,1)S(1)}, bf16[512,512]{1,0:T(8,128)(2,1)S(1)}, u32[]{:S(2)}, u32[]{:S(2)}) collective-permute-start(bf16[512,512]{1,0:T(8,128)(2,1)S(1)} %collective-permute-done.4.refs_3_), channel_id=1, source_target_pairs={{0,32},{32,64},{64,96},{96,128},{128,160},{160,192},{192,224},{224... | collective-permute-start | bytes 1572872 | tf_op jit(solution)/shard_map/ppermute | solution.py:334
  51.3 14.4 %collective-permute-start.7 = (bf16[512,512]{1,0:T(8,128)(2,1)S(1)}, bf16[512,512]{1,0:T(8,128)(2,1)S(1)}, u32[]{:S(2)}, u32[]{:S(2)}) collective-permute-start(bf16[512,512]{1,0:T(8,128)(2,1)S(1)} %collective-permute-done.5.refs_4_), channel_id=1, source_target_pairs={{32,0},{64,32},{96,64},{128,96},{160,128},{192,160},{224,192},{0,2... | collective-permute-start | bytes 1572872 | tf_op jit(solution)/shard_map/ppermute | solution.py:334
  63.7 5.0 %collective-permute-start.10 = (bf16[2,256,512]{2,1,0:T(8,128)(2,1)S(1)}, bf16[2,256,512]{2,1,0:T(8,128)(2,1)S(1)}, u32[]{:S(2)}, u32[]{:S(2)}) collective-permute-start(bf16[2,256,512]{2,1,0:T(8,128)(2,1)S(1)} %collective-permute-done.8.last), channel_id=1, source_target_pairs={{0,1},{1,0},{2,3},{3,2},{4,5},{5,4},{6,7},{7,6},{8,9},{9,8},{10,11... | collective-permute-start | bytes 1572872 | tf_op jit(solution)/shard_map/ppermute | solution.py:359
  65.7 10.1 %collective-permute-start.11 = (bf16[256,512]{1,0:T(8,128)(2,1)S(1)}, bf16[256,512]{1,0:T(8,128)(2,1)S(1)}, u32[]{:S(2)}, u32[]{:S(2)}) collective-permute-start(bf16[256,512]{1,0:T(8,128)(2,1)S(1)} %slice.22), channel_id=1, source_target_pairs={{0,32},{32,64},{64,96},{96,128},{128,160},{160,192},{192,224},{224... | collective-permute-start | bytes 786440 | tf_op jit(solution)/shard_map/ppermute | solution.py:334
  66.0 9.8 %collective-permute-start.12 = (bf16[256,512]{1,0:T(8,128)(2,1)S(1)}, bf16[256,512]{1,0:T(8,128)(2,1)S(1)}, u32[]{:S(2)}, u32[]{:S(2)}) collective-permute-start(bf16[256,512]{1,0:T(8,128)(2,1)S(1)} %slice.23), channel_id=1, source_target_pairs={{32,0},{64,32},{96,64},{128,96},{160,128},{192,160},{224,192},{0,2... | collective-permute-start | bytes 786440 | tf_op jit(solution)/shard_map/ppermute | solution.py:334
  73.0 7.4 %collective-permute-start.13 = (bf16[256,512]{1,0:T(8,128)(2,1)S(1)}, bf16[256,512]{1,0:T(8,128)(2,1)S(1)}, u32[]{:S(2)}, u32[]{:S(2)}) collective-permute-start(bf16[256,512]{1,0:T(8,128)(2,1)S(1)} %get-tuple-element.75), channel_id=1, source_target_pairs={{0,32},{32,64},{64,96},{96,128},{128,160},{160,192},{192,224},{224... | collective-permute-start | bytes 786440 | tf_op jit(solution)/shard_map/ppermute | solution.py:334
  73.1 8.3 %collective-permute-start.14 = (bf16[256,512]{1,0:T(8,128)(2,1)S(1)}, bf16[256,512]{1,0:T(8,128)(2,1)S(1)}, u32[]{:S(2)}, u32[]{:S(2)}) collective-permute-start(bf16[256,512]{1,0:T(8,128)(2,1)S(1)} %get-tuple-element.78), channel_id=1, source_target_pairs={{32,0},{64,32},{96,64},{128,96},{160,128},{192,160},{224,192},{0,2... | collective-permute-start | bytes 786440 | tf_op jit(solution)/shard_map/ppermute | solution.py:334
  82.4 12.4 %collective-permute-start.15 = (bf16[512,512]{1,0:T(8,128)(2,1)}, bf16[512,512]{1,0:T(8,128)(2,1)}, u32[]{:S(2)}, u32[]{:S(2)}) collective-permute-start(bf16[512,512]{1,0:T(8,128)(2,1)} %pad_maximum_fusion.1), channel_id=1, source_target_pairs={{0,32},{32,64},{64,96},{96,128},{128,160},{160,192},{192,224},{224... | collective-permute-start | bytes 1572872 | tf_op jit(solution)/shard_map/ppermute | solution.py:334
  82.4 14.6 %collective-permute-start.16 = (bf16[512,512]{1,0:T(8,128)(2,1)}, bf16[512,512]{1,0:T(8,128)(2,1)}, u32[]{:S(2)}, u32[]{:S(2)}) collective-permute-start(bf16[512,512]{1,0:T(8,128)(2,1)} %pad_maximum_fusion.2), channel_id=1, source_target_pairs={{32,0},{64,32},{96,64},{128,96},{160,128},{192,160},{224,192},{0,2... | collective-permute-start | bytes 1572872 | tf_op jit(solution)/shard_map/ppermute | solution.py:334
  85.0 24.6 %all-to-all-start.2 = ((bf16[32,32,512]{2,1,0:T(8,128)(2,1)}), bf16[32,32,512]{2,1,0:T(8,128)(2,1)S(1)}, u32[]{:S(2)}, u32[]{:S(2)}) async-start(bf16[32,32,512]{2,1,0:T(8,128)(2,1)} %bitcast.22), calls=%async_computation.2 | async-start | bytes 2097152 | tf_op jit(solution)/shard_map/all_to_all | solution.py:378
  98.9 16.2 %collective-permute-start.17 = (bf16[512,512]{1,0:T(8,128)(2,1)}, bf16[512,512]{1,0:T(8,128)(2,1)}, u32[]{:S(2)}, u32[]{:S(2)}) collective-permute-start(bf16[512,512]{1,0:T(8,128)(2,1)} %add_convert_fusion.3), channel_id=1, source_target_pairs={{0,32},{32,64},{64,96},{96,128},{128,160},{160,192},{192,224},{224... | collective-permute-start | bytes 1572872 | tf_op jit(solution)/shard_map/ppermute | solution.py:334
  98.9 18.3 %collective-permute-start.18 = (bf16[512,512]{1,0:T(8,128)(2,1)}, bf16[512,512]{1,0:T(8,128)(2,1)}, u32[]{:S(2)}, u32[]{:S(2)}) collective-permute-start(bf16[512,512]{1,0:T(8,128)(2,1)} %add_convert_fusion.2), channel_id=1, source_target_pairs={{32,0},{64,32},{96,64},{128,96},{160,128},{192,160},{224,192},{0,2... | collective-permute-start | bytes 1572872 | tf_op jit(solution)/shard_map/ppermute | solution.py:334
  111.0 14.0 %all-to-all-start.3 = ((bf16[16,32,512]{2,1,0:T(8,128)(2,1)}), bf16[16,32,512]{2,1,0:T(8,128)(2,1)S(1)}, u32[]{:S(2)}, u32[]{:S(2)}) async-start(bf16[16,32,512]{2,1,0:T(8,128)(2,1)} %bitcast.11), calls=%async_computation.3 | async-start | bytes 1048576 | tf_op jit(solution)/shard_map/all_to_all | solution.py:379
  119.2 13.6 %collective-permute-start.20 = (bf16[512,512]{1,0:T(8,128)(2,1)}, bf16[512,512]{1,0:T(8,128)(2,1)S(1)}, u32[]{:S(2)}, u32[]{:S(2)}) collective-permute-start(bf16[512,512]{1,0:T(8,128)(2,1)} %add_convert_fusion), channel_id=1, source_target_pairs={{32,0},{64,32},{96,64},{128,96},{160,128},{192,160},{224,192},{0,2... | collective-permute-start | bytes 1572872 | tf_op jit(solution)/shard_map/ppermute | solution.py:334
  119.6 14.5 %collective-permute-start.19 = (bf16[512,512]{1,0:T(8,128)(2,1)}, bf16[512,512]{1,0:T(8,128)(2,1)}, u32[]{:S(2)}, u32[]{:S(2)}) collective-permute-start(bf16[512,512]{1,0:T(8,128)(2,1)} %add_convert_fusion.1), channel_id=1, source_target_pairs={{0,32},{32,64},{64,96},{96,128},{128,160},{160,192},{192,224},{224... | collective-permute-start | bytes 1572872 | tf_op jit(solution)/shard_map/ppermute | solution.py:334
  (17 other events, 91.0 us)
